TPU v7x, 32 devices: a whole 2x2x4 slice. The times are simulated.
32 devices in a mesh: segment: 4 (over y, x), dom: 8 (over z, core).
Axes of the slice: x: 2, y: 2, z: 4, core: 2. Of those that a mesh axis runs over, the one named last changes fastest.
Arguments:
- features: bfloat16 [4, 4096, 512], P(None, 'dom'), may hold values from -6 to 6
- layer_weights: bfloat16 [8, 1024, 512], P('segment'), may hold values from -0.1875 to 0.1875
- layer_bias: float32 [8, 512], P('segment'), may hold values from -3 to 3
- layer_gain: float32 [8, 512], P('segment'), may hold values from 0.1 to 1.9
- tile_val: bfloat16 [32, 4, 128, 128], P('dom'), may hold values from -0.25 to 0.25
- tile_col: int32 [32, 4], P('dom'), may hold values from 0 to 3
- tile_count: int32 [32], P('dom'), may hold values from 1 to 4, as said below
- cross_val: bfloat16 [8, 32, 128, 128], P('segment', 'dom'), may hold values from -0.5 to 0.5
- send_rows: int32 [8, 1024], P('segment', 'dom'), may hold values from 0 to 511, as said below
Outputs:
- segment_out: bfloat16 [4, 4, 4096, 512], P('segment', None, 'dom')
Inputs may be any that keep to these rules, and one draw needn't show every extreme that they name: `tile_count`: in some row block of the graph all 4 slots are live. `send_rows`: each partition's list at a layer holds 128 distinct local node indices and contains 512 - 1.
All inputs are finite; a program needn't handle non-finite values.
Results may differ from a plain program's by a relative error of at most 0.012.
Values may be sent and summed in bfloat16 or wider, within the bound.
No kernel may reach another device: no remote copies, remote signals or barrier semaphores. Data moves between devices by JAX's collectives and lax.ppermute only.
A program may use at most 64 MiB of HBM per device.

v0:
```python
import functools

import jax
import jax.numpy as jnp
from jax import lax
from jax.experimental import pallas as pl
from jax.experimental.pallas import tpu as pltpu
from jax.sharding import PartitionSpec as P

F32 = jnp.float32
BF16 = jnp.bfloat16
VMEM_BYTES = 12 * 2**20
LOAD = 0.5
VM = pl.BlockSpec(memory_space=pltpu.VMEM)
SM = pl.BlockSpec(memory_space=pltpu.SMEM)
ANY = pl.BlockSpec(memory_space=pl.ANY)
HBM = pl.BlockSpec(memory_space=pltpu.HBM)


def call(body, outs, in_specs, scratch=(), out_specs=None, flops=0, vmem=VMEM_BYTES):
    if out_specs is None:
        out_specs = jax.tree.map(lambda _: VM, outs)
    inner = body.func if isinstance(body, functools.partial) else body
    return pl.pallas_call(
        body,
        name=inner.__name__,
        out_shape=outs,
        in_specs=in_specs,
        out_specs=out_specs,
        scratch_shapes=scratch,
        compiler_params=pltpu.CompilerParams(vmem_limit_bytes=vmem),
        cost_estimate=pl.CostEstimate(flops=int(flops), bytes_accessed=0, transcendentals=0),
    )


def position():
    return lax.axis_index("segment"), lax.axis_index("dom") & 1


def dot(a, b):
    return jnp.dot(a, b, preferred_element_type=F32)


def aligned(start, unit):
    return start if isinstance(start, int) else pl.multiple_of(start, unit)


def normed(hf, gain):
    meansq = jnp.mean(hf * hf, axis=-1, keepdims=True)
    return (hf * lax.rsqrt(meansq + 1e-05) * gain).astype(BF16)


def stepped(h, z):
    half = 0.5 * z
    return (h.astype(F32) + half + half * jnp.tanh(half)).astype(BF16)


def start_one(choices, dst, sem):
    for condition, source in choices:

        @pl.when(condition)
        def _():
            pltpu.make_async_copy(source, dst, sem).start()

    return pltpu.make_async_copy(choices[0][1], dst, sem)


def source_of(seg, section, half):
    near, far = 1 + half, 2 - half
    via = seg ^ far
    passed = jnp.logical_or(via == 1, via == 2)
    second = jnp.where(passed, seg ^ 3, via)
    return jnp.where(seg == section, 0, jnp.where((seg ^ near) == section, 1, jnp.where(second == section, 2, 3)))


def fetch_half(seg, core, section, half, own, mine, theirs, dst, sem):
    width = dst.shape[1]
    source = source_of(seg, section, half)
    choices = [(source == 0, own.at[pl.ds(half * width, width), :])]
    for here, refs in ((core == half, mine), (core != half, theirs)):
        for i, ref in enumerate(refs):
            choices.append((jnp.logical_and(here, source == i + 1), ref.at[pl.ds(0, width), :]))
    return [start_one(choices, dst, sem)]


def fetch_cross(seg, core, section, own, mine, dst, sems):
    tile = dst.shape[0]
    width = dst.shape[1]
    blocks = own.shape[0]
    source = jnp.where(core == 0, source_of(seg, section, 0), source_of(seg, section, 1))
    for i, ref in enumerate(mine):

        @pl.when(source == i + 1)
        def _():
            for b in range(blocks):
                part = ref.at[pl.ds(width, tile), pl.ds(b * tile, tile)]
                pltpu.make_async_copy(part, dst.at[:, pl.ds(b * tile, tile)], sems.at[b]).start()

    @pl.when(source == 0)
    def _():
        for b in range(blocks):
            pltpu.make_async_copy(own.at[b], dst.at[:, pl.ds(b * tile, tile)], sems.at[b]).start()

    return [pltpu.make_async_copy(own.at[b], dst.at[:, pl.ds(b * tile, tile)], sems.at[b]) for b in range(blocks)]


def fetch_layer(section, step, ids, cands, top, bottom, cross, sems):
    own, own_cross, mine, theirs = cands
    seg, core = ids[0], ids[1]
    return (
        fetch_half(seg, core, section, 0, own.at[step], mine, theirs, top, sems.at[0])
        + fetch_half(seg, core, section, 1, own.at[step], mine, theirs, bottom, sems.at[1])
        + fetch_cross(seg, core, section, own_cross.at[step], mine, cross, sems.at[pl.ds(2, own_cross.shape[1])])
    )


def cands_of(refs):
    n = (len(refs) - 2) // 2
    return refs[0], refs[1], refs[2 : 2 + n], refs[2 + n :]


def first_kernel(dep, cols, counts, feat_ref, tiles_ref, s0, s1, s2, s3, h_ref, adj_ref, x_ref, sent_ref, small_ref, pick_ref, sem):
    ids = position()
    nblk, slots, tile, _ = tiles_ref.shape
    nodes, width = h_ref.shape
    seg = ids[0]
    copy = pltpu.make_async_copy(feat_ref.at[seg], h_ref, sem)
    copy.start()
    for r in range(nblk):
        for j in range(nblk):
            total = jnp.zeros((tile, tile), F32)
            for k in range(slots):
                used = jnp.logical_and(k < counts[r], cols[r, k] == j)
                total = total + jnp.where(used, tiles_ref[r, k].astype(F32), 0.0)
            adj_ref[r * tile : (r + 1) * tile, j * tile : (j + 1) * tile] = total.astype(BF16)
    for r, ref in enumerate((s0, s1, s2, s3)):
        small_ref[seg ^ r] = ref[...]
    sections, steps = small_ref.shape[:2]
    bound = small_ref.shape[2] - 2 * width
    for k in range(sections):
        for p in range(steps):
            rows = small_ref[k, p : p + 1, 2 * width :]
            index = lax.broadcasted_iota(jnp.int32, (nodes, bound), 0).astype(F32)
            pick_ref[k, p] = jnp.where(index == rows, 1.0, 0.0).T.astype(BF16)
    copy.wait()
    x = normed(h_ref[...].astype(F32), small_ref[0, 0:1, width : 2 * width])
    x_ref[...] = x
    sent_ref[...] = dot(pick_ref[0, 0], x).astype(BF16)


def payload_kernel(own, cross, *refs):
    outs, sems = refs[:-1], refs[-1]
    copies = []
    for p, out_ref in enumerate(outs):
        width = out_ref.shape[1]
        tile = cross.shape[-1]
        copies.append(pltpu.make_async_copy(own.at[p], out_ref.at[pl.ds(0, width), :], sems.at[p, 0]))
        for b in range(cross.shape[1]):
            dst = out_ref.at[pl.ds(width, tile), pl.ds(b * tile, tile)]
            copies.append(pltpu.make_async_copy(cross.at[p, b], dst, sems.at[p, b + 1]))
    for copy in copies:
        copy.start()
    for copy in copies:
        copy.wait()


def select_kernel(wanted, *refs):
    ids = position()
    count = len(wanted)
    outs, sources = refs[-count:], refs
    rows = sources[0].shape[0]
    for out_ref, rule in zip(outs, wanted):
        if out_ref.shape[0] > rows:
            out_ref[rows:, :] = jnp.zeros((out_ref.shape[0] - rows, out_ref.shape[1]), out_ref.dtype)
        for i, segments in enumerate(rule):
            here = functools.reduce(jnp.logical_or, [ids[0] == s for s in segments])

            @pl.when(here)
            def _():
                out_ref[:rows, :] = sources[i][...]


def select(sources, wanted, deps=(), extra=0):
    rows, columns = sources[0].shape
    shape = jax.ShapeDtypeStruct((rows + extra, columns), sources[0].dtype)
    specs = [VM] * len(sources) + [ANY] * len(deps)
    return call(functools.partial(select_kernel, wanted), [shape] * len(wanted), specs, vmem=8 * 2**20)(*sources, *deps)


def tie(value, *deps):
    return pl.pallas_call(
        lambda *refs: None,
        name="tie",
        out_shape=jax.ShapeDtypeStruct(value.shape, value.dtype),
        in_specs=[ANY] * (1 + len(deps)),
        out_specs=ANY,
        input_output_aliases={0: 0},
        compiler_params=pltpu.CompilerParams(vmem_limit_bytes=2**20),
    )(value, *deps)


def top_kernel(dep, in_ref, out_ref):
    out_ref[...] = in_ref[: out_ref.shape[0], :]


def load_kernel(section, dep, *refs):
    ids = position()
    w_ref, c_ref, sems = refs[-3:]
    width = w_ref.shape[1]
    parts = w_ref.at[pl.ds(0, width), :], w_ref.at[pl.ds(width, width), :]
    for copy in fetch_layer(section, 0, ids, cands_of(refs[:-3]), *parts, c_ref, sems):
        copy.wait()


def edge_kernel(section, x_ref, h_ref, adj_ref, w_ref, c_ref, small_ref, pick_ref, agg_ref, z_ref, cross_ref, h_out):
    width = x_ref.shape[1]
    pick = pick_ref[section, 1]
    x = x_ref[...]
    adj = dot(pick, adj_ref[...]).astype(BF16)
    agg_ref[...] = dot(adj, x)
    xb = dot(pick, x).astype(BF16)
    z_ref[...] = dot(xb, w_ref[:width, :]) + small_ref[section, 0:1, :width]
    tile = c_ref.shape[0]
    cross = jnp.zeros((pick.shape[0], tile), F32)
    for b in range(c_ref.shape[1] // tile):
        lanes = slice(b * tile, (b + 1) * tile)
        cross = cross + dot(pick[:, lanes], c_ref[:, lanes])
    cross_ref[...] = cross.astype(BF16)
    h_out[...] = dot(pick, h_ref[...]).astype(BF16)


def send_kernel(section, recv_ref, agg_ref, z_ref, cross_ref, h_ref, w_ref, small_ref, sent_ref):
    width = h_ref.shape[1]
    agg = (agg_ref[...] + dot(cross_ref[...], recv_ref[...])).astype(BF16)
    z = z_ref[...] + dot(agg, w_ref[width:, :])
    h = stepped(h_ref[...], z)
    sent_ref[...] = normed(h.astype(F32), small_ref[section, 1:2, width : 2 * width])


def remote(c_ref, recv, i, block):
    tile = c_ref.shape[0]
    parts = []
    for b in range(block // tile):
        lanes = pl.ds(aligned(i * block + b * tile, tile), tile)
        parts.append(dot(c_ref[:, lanes], recv))
    return jnp.concatenate(parts, axis=0)


def even_kernel(section, x_ref, h_ref, adj_ref, recv_ref, w_ref, c_ref, small_ref, dep, h_out, x_out):
    nodes, width = x_ref.shape
    block = 256

    def even(i, carry):
        rows = pl.ds(aligned(i * block, block), block)
        agg = dot(adj_ref[rows, :], x_ref[...]) + remote(c_ref, recv_ref[...], i, block)
        z = dot(x_ref[rows, :], w_ref[:width, :]) + small_ref[section, 0:1, :width]
        z = z + dot(agg.astype(BF16), w_ref[width:, :])
        h = stepped(h_ref[rows, :], z)
        h_out[rows, :] = h
        x_out[rows, :] = normed(h.astype(F32), small_ref[section, 1:2, width : 2 * width])
        return carry

    lax.fori_loop(0, nodes // block, even, 0)


def odd_kernel(section, fetch, dep, x_ref, adj_ref, small_ref, *refs):
    ids = position()
    if fetch:
        z_out, w2_out, c_out, w_out, next_c_out, w1_ref, sems, next_sems = refs[-8:]
        cands, ahead = refs[: fetch], refs[fetch:-8]
    else:
        z_out, w2_out, c_out, w1_ref, sems = refs[-5:]
        cands = refs[:-5]
    nodes, width = x_ref.shape
    block = 256
    copies = fetch_layer(section, 1, ids, cands_of(cands), w1_ref, w2_out, c_out, sems)
    if fetch:
        parts = w_out.at[pl.ds(0, width), :], w_out.at[pl.ds(width, width), :]
        copies += fetch_layer(section + 1, 0, ids, cands_of(ahead), *parts, next_c_out, next_sems)
    copies[0].wait()
    copies[1].wait()

    def odd(i, carry):
        rows = pl.ds(aligned(i * block, block), block)
        agg = dot(adj_ref[rows, :], x_ref[...]).astype(BF16)
        z = dot(x_ref[rows, :], w1_ref[...]) + small_ref[section, 1:2, :width]
        z_out[rows, :] = z + dot(agg, w2_out[...])
        return carry

    lax.fori_loop(0, nodes // block, odd, 0)
    for copy in copies[2:]:
        copy.wait()


def finish_kernel(section, last, recv_ref, z_ref, w2_ref, c_ref, h_ref, small_ref, pick_ref, *refs):
    nodes, width = h_ref.shape
    block = 256
    ids = position()
    if last:
        ends, (h_out, *pays) = refs[:section], refs[section:]
        for k, end_ref in enumerate(ends):
            for r, pay_ref in enumerate(pays, 1):

                @pl.when(ids[0] == k ^ r)
                def _():
                    pay_ref[:nodes, :] = end_ref[...]

        for pay_ref in pays:
            pay_ref[nodes:, :] = jnp.zeros((pay_ref.shape[0] - nodes, width), BF16)
    else:
        h_out, x_out, sent_out = refs
    seen = dot(recv_ref[...], w2_ref[...]).astype(BF16)
    for i in range(nodes // block):
        rows = pl.ds(i * block, block)
        z = z_ref[rows, :] + remote(c_ref, seen, i, block)
        h = stepped(h_ref[rows, :], z)
        h_out[rows, :] = h
        if last:
            for r, pay_ref in enumerate(pays, 1):

                @pl.when(ids[0] == section ^ r)
                def _():
                    pay_ref[rows, :] = h
        else:
            x_out[rows, :] = normed(h.astype(F32), small_ref[section + 1, 0:1, width : 2 * width])
    if not last:
        sent_out[...] = dot(pick_ref[section + 1, 0], x_out[...]).astype(BF16)


def collect_early_kernel(*refs):
    ids = position()
    out_ref, sem = refs[-2:]
    start_one([(ids[0] == k, end) for k, end in enumerate(refs[:-2])], out_ref.at[0, ids[0]], sem).wait()


def collect_last_kernel(one_ref, two_ref, three_ref, first_ref, early_ref, later_ref, _, out_ref, sems):
    ids = position()
    last = out_ref.shape[1] - 1
    rows = pl.ds(0, out_ref.shape[2])
    copies = [
        pltpu.make_async_copy(ref.at[rows, :], out_ref.at[0, ids[0] ^ r], sems.at[r]) for r, ref in ((1, one_ref), (2, two_ref))
    ]
    for copy in copies:
        copy.start()
    choices = [
        (ids[0] == last, three_ref),
        (ids[0] < 2, first_ref.at[rows, :]),
        (jnp.logical_and(ids[0] == 2, ids[1] == 0), early_ref.at[rows, :]),
        (jnp.logical_and(ids[0] == 2, ids[1] != 0), later_ref.at[rows, :]),
    ]
    copies.append(start_one(choices, out_ref.at[0, ids[0] ^ 3], sems.at[3]))
    for copy in copies:
        copy.wait()


def shards(features, weights, bias, gain, tile_val, tile_col, tile_count, cross_val, send_rows):
    sections = lax.axis_size("segment")
    doms = lax.axis_size("dom")
    seg = lax.axis_index("segment")
    core = lax.axis_index("dom") & 1
    steps, _, width = weights.shape
    nodes = features.shape[1]
    bound = send_rows.shape[1]
    nbits = doms.bit_length() - 1

    def moved(value, target, sources=range(sections)):
        pairs = []
        for s in sources:
            for d in range(doms):
                t, e = target(s, d)
                pairs.append((s * doms + d, t * doms + e))
        return lax.ppermute(value, ("segment", "dom"), pairs)

    def near(s, d):
        return s ^ (1 + (d & 1)), d

    def far(s, d):
        return s ^ (2 - (d & 1)), d

    def sibling(s, d):
        return s, d ^ 1

    def across(r):
        return lambda s, d: (s ^ r, d)

    def exchange(sent, step):
        bit = step * (nbits - 1) // max(steps - 1, 1)
        return lax.ppermute(sent, "dom", [(i, i ^ 1 << bit) for i in range(doms)])

    mat = jax.ShapeDtypeStruct((nodes, width), BF16)
    mat32 = jax.ShapeDtypeStruct((nodes, width), F32)
    tall = jax.ShapeDtypeStruct((nodes + 32, width), BF16)
    edge = jax.ShapeDtypeStruct((bound, width), BF16)
    edge32 = jax.ShapeDtypeStruct((bound, width), F32)
    half = jax.ShapeDtypeStruct((width, width), BF16)
    both = jax.ShapeDtypeStruct((2 * width, width), BF16)
    load = jax.ShapeDtypeStruct((width + bound, width), BF16)
    picks = jax.ShapeDtypeStruct((sections, steps, bound, nodes), BF16)
    unit = 2 * nodes * width * width
    dmas = pltpu.SemaphoreType.DMA((2 + cross_val.shape[1],))

    own = call(
        payload_kernel,
        [load] * steps,
        [ANY, ANY],
        scratch=[pltpu.SemaphoreType.DMA((steps, 1 + cross_val.shape[1]))],
    )(lax.dynamic_slice_in_dim(weights, core * width, width, axis=1), cross_val)
    small = tie(jnp.concatenate([bias, gain, send_rows.astype(F32)], axis=1), own[0])
    smalls = [small] + [moved(small, across(r)) for r in range(1, sections)]
    inner, outer = (1, 2), (0, 3)
    a0, a1 = [moved(v, near) for v in own]
    (pay,) = select([a0, own[0]], [(inner, outer)])
    b0 = moved(pay, far)
    (pay,) = select([a1, own[1]], [(inner, outer)], [pay, *smalls[1:]])
    b1 = moved(pay, far)
    issued = pay
    (pay,) = select([own[0], a0], [(inner, outer)], [pay])
    c0 = moved(pay, far)
    (pay,) = select([own[1], a1], [(inner, outer)], [pay])
    c1 = moved(pay, far)
    h, adj, x, sent, small, pick = call(
        first_kernel,
        (mat, jax.ShapeDtypeStruct((nodes, nodes), BF16), mat, edge, jax.ShapeDtypeStruct((sections,) + small.shape, F32), picks),
        [ANY, SM, SM, HBM, VM] + [VM] * sections,
        scratch=[pltpu.SemaphoreType.DMA],
    )(issued, tile_col, tile_count, features, tile_val, *smalls)
    recv = exchange(sent, 0)

    sa0 = moved(call(top_kernel, half, [ANY, VM])(issued, a0), sibling)
    sb0 = moved(call(top_kernel, half, [ANY, VM])(issued, b0), sibling)
    brought, swapped = [[a0, b0], [a1]], [[sa0, sb0], []]

    def candidates(p):
        return [weights, cross_val, *brought[p], *swapped[p]]

    def loaded(section, dep):
        cands = candidates(0)
        specs = [ANY, HBM, HBM] + [ANY] * (len(cands) - 2)
        kernel = functools.partial(load_kernel, section)
        return call(kernel, (both, edge), specs, scratch=[dmas])(dep, *cands)

    w, c = loaded(0, pay)

    ends = []
    last_segment = sections - 1
    for k in range(sections):
        last = k == sections - 1
        if k > 0:
            recv = exchange(sent, 0)
        if k == 1:
            c1 = tie(c1, x)
            w, c = loaded(1, c1)
        edges = call(
            functools.partial(edge_kernel, k),
            (edge32, edge32, jax.ShapeDtypeStruct((bound, bound), BF16), edge),
            [VM] * 7,
            flops=LOAD * unit / 4,
        )(x, h, adj, w, c, small, pick)
        sent = call(functools.partial(send_kernel, k), edge, [VM] * 7, flops=LOAD * unit / 4)(recv, *edges[:3], edges[3], w, small)
        recv2 = exchange(sent, 1)
        if k == 1:
            brought[1].append(c1)
            swapped[1].append(moved(brought[1][2], sibling))
        h, x = call(functools.partial(even_kernel, k), (mat, mat), [VM] * 7 + [ANY], flops=LOAD * unit)(
            x, h, adj, recv, w, c, small, sent
        )
        if k == 0:
            brought[1] = [tie(a1, sent), tie(b1, sent)]
            swapped[1] = [moved(v, sibling) for v in brought[1]]
        cands = candidates(1)
        ahead = candidates(0) if k in range(1, sections - 1) else []
        fetch = len(cands) if ahead else 0
        specs = [([HBM, HBM] + [ANY] * (len(v) - 2) if v else []) for v in (cands, ahead)]
        z, w2, c2, *loads = call(
            functools.partial(odd_kernel, k, fetch),
            (mat32, half, edge) + ((both, edge) if ahead else ()),
            [ANY] + [VM] * 3 + specs[0] + specs[1],
            scratch=[pltpu.VMEM((width, width), BF16), dmas] + ([dmas] if ahead else []),
            flops=(20 if k > 1 else LOAD) * unit,
        )(c0 if k == 0 else first_two if last else x, x, adj, small, *cands, *ahead)
        if k == 0:
            brought[0].append(tie(c0, recv2, z))
            swapped[0].append(moved(brought[0][2], sibling))
        if k == 2:
            (pay,) = select(ends, [[(j ^ 3,) for j in range(2)]], [x], extra=16)
            first_two = moved(pay, across(3), [j ^ 3 for j in range(2)])
        if last:
            (pay,) = select(ends[2:], [[(2 ^ 3,)]], [x], extra=16)
            others = [2 ^ 3]
            early = moved(pay, lambda s, d: (s ^ (2 if d & 1 else 3), d), others)
        out = call(
            functools.partial(finish_kernel, k, last),
            (mat, tall, tall) if last else (mat, mat, edge),
            [VM] * 7 + ([VM] * len(ends) if last else []),
            flops=LOAD * unit,
        )(recv2, z, w2, c2, h, small, pick, *(ends if last else []))
        ends.append(out[0])
        if not last:
            h, x, sent = out
        if ahead:
            w, c = loads
    hop = moved(ends[-1], near, [last_segment ^ 3])
    two = moved(out[2], across(2))
    one = moved(out[1], across(1))
    def onward(value, between, sources, parity=None):
        pairs = []
        for s in sources:
            for d in range(doms):
                if parity is None or d & 1 == parity:
                    pairs.append((between(s, d) * doms + d, (s ^ 3) * doms + d))
        return lax.ppermute(value, ("segment", "dom"), pairs)

    three = onward(tie(hop, early), lambda s, d: near(s, d)[0], [last_segment ^ 3])
    later = onward(early, lambda s, d: s ^ 2, others, 1)
    whole = jax.ShapeDtypeStruct((1, sections, nodes, width), BF16)
    sems = [pltpu.SemaphoreType.DMA((sections,))]
    partly = call(
        collect_early_kernel, whole, [ANY] * sections, scratch=[pltpu.SemaphoreType.DMA], out_specs=ANY
    )(*ends)
    return pl.pallas_call(
        collect_last_kernel,
        name="collect_last_kernel",
        out_shape=whole,
        in_specs=[ANY] * 7,
        out_specs=ANY,
        scratch_shapes=sems,
        input_output_aliases={6: 0},
        compiler_params=pltpu.CompilerParams(vmem_limit_bytes=2**20),
    )(one, two, three, first_two, early, later, partly)


def solution(mesh):
    in_specs = (
        P(None, "dom", None),
        P("segment", None, None),
        P("segment", None),
        P("segment", None),
        P("dom", None, None, None),
        P("dom", None),
        P("dom"),
        P("segment", "dom", None, None),
        P("segment", "dom"),
    )
    out_specs = P("segment", None, "dom", None)
    return jax.shard_map(shards, mesh=mesh, in_specs=in_specs, out_specs=out_specs, check_vma=False)
```

profile of v0, /device:TPU:6, one launch (start us, length us, event | category | flops | bytes accessed | tf_op | source)
XLA Modules:
  0.0 113.8 jit_solution(14011935346687299620)
XLA Ops:
  0.0 1.3 %constant_dynamic-slice_fusion.own = bf16[2,512,512]{2,1,0:T(8,128)(2,1)S(1)} fusion(bf16[2,1024,512]{2,1,0:T(8,128)(2,1)} %refs_0_.11, s32[]{:T(128)S(6)} %select_n.3), kind=kLoop, calls=%fused_computation.1 | loop fusion | bytes 2097156 | tf_op jit(solution)/shard_map/dynamic_slice | solution.py:407
  2.2 1.5 %collective-permute-start = (bf16[640,512]{1,0:T(8,128)(2,1)S(1)}, bf16[640,512]{1,0:T(8,128)(2,1)S(1)}, u32[]{:S(2)}, u32[]{:S(2)}) collective-permute-start(bf16[640,512]{1,0:T(8,128)(2,1)S(1)} %get-tuple-element.69.refs_1_.refs_0_), channel_id=1, source_target_pairs={{0,8},{1,17},{2,10},{3,19},{4,12},{5,21},{6,14},{7,23},{8,0},{9,25... | collective-permute-start | bytes 1966088 | tf_op jit(solution)/shard_map/ppermute | solution.py:372
  3.7 8.6 %collective-permute-done.1.refs_0_.refs_1_.in_ref.refs_2_.refs_10_ = bf16[640,512]{1,0:T(8,128)(2,1)S(1)} collective-permute-done((bf16[640,512]{1,0:T(8,128)(2,1)S(1)}, bf16[640,512]{1,0:T(8,128)(2,1)S(1)}, u32[]{:S(2)}, u32[]{:S(2)}) %collective-permute-start.1) | collective-permute-done | bytes 655392 | tf_op jit(solution)/shard_map/ppermute | solution.py:372
  12.9 1.6 %collective-permute-start.4 = (f32[2,1152]{1,0:T(2,128)S(1)}, f32[2,1152]{1,0:T(2,128)S(1)}, u32[]{:S(2)}, u32[]{:S(2)}) collective-permute-start(f32[2,1152]{1,0:T(2,128)S(1)} %tie.6.s0), channel_id=1, source_target_pairs={{0,24},{1,25},{2,26},{3,27},{4,28},{5,29},{6,30},{7,31},{8,16},{9,... | collective-permute-start | bytes 27656 | tf_op jit(solution)/shard_map/ppermute | solution.py:372
  14.6 1.9 %collective-permute-start.2 = (f32[2,1152]{1,0:T(2,128)S(1)}, f32[2,1152]{1,0:T(2,128)S(1)}, u32[]{:S(2)}, u32[]{:S(2)}) collective-permute-start(f32[2,1152]{1,0:T(2,128)S(1)} %tie.6.s0), channel_id=1, source_target_pairs={{0,8},{1,9},{2,10},{3,11},{4,12},{5,13},{6,14},{7,15},{8,0},{9,1},... | collective-permute-start | bytes 27656 | tf_op jit(solution)/shard_map/ppermute | solution.py:372
  16.5 8.2 %collective-permute-done.4.refs_5_.s3 = f32[2,1152]{1,0:T(2,128)S(1)} collective-permute-done((f32[2,1152]{1,0:T(2,128)S(1)}, f32[2,1152]{1,0:T(2,128)S(1)}, u32[]{:S(2)}, u32[]{:S(2)}) %collective-permute-start.4) | collective-permute-done | bytes 9248 | tf_op jit(solution)/shard_map/ppermute | solution.py:372
  27.2 1.8 %first_kernel.1 = (bf16[512,512]{1,0:T(8,128)(2,1)S(1)}, bf16[512,512]{1,0:T(8,128)(2,1)S(1)}, bf16[512,512]{1,0:T(8,128)(2,1)S(1)}, bf16[128,512]{1,0:T(8,128)(...) custom-call(bf16[640,512]{1,0:T(8,128)(2,1)S(1)} %select_kernel.7.dep.refs_2_, ...), custom_call_target="tpu_custom_call" | custom-call | tf_op jit(solution)/shard_map/first_kernel/pallas_call | solution.py:421
  30.2 1.5 %collective-permute-start.10 = (bf16[640,512]{1,0:T(8,128)(2,1)S(1)}, bf16[640,512]{1,0:T(8,128)(2,1)S(1)}, u32[]{:S(2)}, u32[]{:S(2)}) collective-permute-start(bf16[640,512]{1,0:T(8,128)(2,1)S(1)} %select_kernel.8.refs_2_), channel_id=1, source_target_pairs={{0,16},{1,9},{2,18},{3,11},{4,20},{5,13},{6,22},{7,15},{8,24},{9,1... | collective-permute-start | bytes 1966088 | tf_op jit(solution)/shard_map/ppermute | solution.py:372
  33.4 2.9 %collective-permute-done.11.refs_0_ = bf16[640,512]{1,0:T(8,128)(2,1)S(1)} collective-permute-done((bf16[640,512]{1,0:T(8,128)(2,1)S(1)}, bf16[640,512]{1,0:T(8,128)(2,1)S(1)}, u32[]{:S(2)}, u32[]{:S(2)}) %collective-permute-start.11) | collective-permute-done | bytes 655392 | tf_op jit(solution)/shard_map/ppermute | solution.py:372
  36.4 1.4 %collective-permute-start.15 = (bf16[640,512]{1,0:T(8,128)(2,1)S(1)}, bf16[640,512]{1,0:T(8,128)(2,1)S(1)}, u32[]{:S(2)}, u32[]{:S(2)}) collective-permute-start(bf16[640,512]{1,0:T(8,128)(2,1)S(1)} %select_kernel.9.dep), channel_id=1, source_target_pairs={{0,16},{1,9},{2,18},{3,11},{4,20},{5,13},{6,22},{7,15},{8,24},{9,1... | collective-permute-start | bytes 1966088 | tf_op jit(solution)/shard_map/ppermute | solution.py:372
  37.8 2.6 %collective-permute-start.9 = (bf16[128,512]{1,0:T(8,128)(2,1)S(1)}, bf16[128,512]{1,0:T(8,128)(2,1)S(1)}, u32[]{:S(2)}, u32[]{:S(2)}) collective-permute-start(bf16[128,512]{1,0:T(8,128)(2,1)S(1)} %send_kernel.4.dep.refs_1_), channel_id=1, source_target_pairs={{0,4},{1,5},{2,6},{3,7},{4,0},{5,1},{6,2},{7,3},{8,12},{9,13},{10,... | collective-permute-start | bytes 393224 | tf_op jit(solution)/shard_map/ppermute | solution.py:388
  40.4 1.8 %even_kernel.4 = (bf16[512,512]{1,0:T(8,128)(2,1)S(1)}, bf16[512,512]{1,0:T(8,128)(2,1)S(1)}) custom-call(bf16[512,512]{1,0:T(8,128)(2,1)S(1)} %get-tuple-element.72.x_ref, bf16[512,512]{1,0:T(8,128)(2,1)S(1)} %get-tuple-element.73.h_ref, bf16[512,512]{1,0:T(8,128)(2,1)S(1)} %get-tuple-element.74.adj_ref, ...), custom_call_target="tpu_custom_call" | custom-call | flops 134217728 | tf_op jit(solution)/shard_map/even_kernel/pallas_call | solution.py:464
  43.3 1.3 %odd_kernel.4 = (f32[512,512]{1,0:T(8,128)S(1)}, bf16[512,512]{1,0:T(8,128)(2,1)S(1)}, bf16[128,512]{1,0:T(8,128)(2,1)S(1)}) custom-call(bf16[640,512]{1,0:T(8,128)(2,1)S(1)} %collective-permute-done.10.dep.refs_0_, bf16[512,512]{1,0:T(8,128)(2,1)S(1)} %get-tuple-element.83.x_ref, bf16[512,512]{1,0:T(8,128)(2,1)S(1)} %get-tuple-element.74.adj_ref, ...), custom_call_target="tpu_custom_call" | custom-call | flops 134217728 | tf_op jit(solution)/shard_map/odd_kernel/pallas_call | solution.py:474
  44.6 1.5 %collective-permute-done.9.recv_ref.refs_1_ = bf16[128,512]{1,0:T(8,128)(2,1)S(1)} collective-permute-done((bf16[128,512]{1,0:T(8,128)(2,1)S(1)}, bf16[128,512]{1,0:T(8,128)(2,1)S(1)}, u32[]{:S(2)}, u32[]{:S(2)}) %collective-permute-start.9) | collective-permute-done | bytes 131104 | tf_op jit(solution)/shard_map/ppermute | solution.py:388
  47.3 3.0 %collective-permute-done.15.refs_0_ = bf16[640,512]{1,0:T(8,128)(2,1)S(1)} collective-permute-done((bf16[640,512]{1,0:T(8,128)(2,1)S(1)}, bf16[640,512]{1,0:T(8,128)(2,1)S(1)}, u32[]{:S(2)}, u32[]{:S(2)}) %collective-permute-start.15) | collective-permute-done | bytes 655392 | tf_op jit(solution)/shard_map/ppermute | solution.py:372
  53.1 2.7 %collective-permute-start.17 = (bf16[128,512]{1,0:T(8,128)(2,1)S(1)}, bf16[128,512]{1,0:T(8,128)(2,1)S(1)}, u32[]{:S(2)}, u32[]{:S(2)}) collective-permute-start(bf16[128,512]{1,0:T(8,128)(2,1)S(1)} %send_kernel.5.dep), channel_id=1, source_target_pairs={{0,4},{1,5},{2,6},{3,7},{4,0},{5,1},{6,2},{7,3},{8,12},{9,13},{10,... | collective-permute-start | bytes 393224 | tf_op jit(solution)/shard_map/ppermute | solution.py:388
  55.7 1.8 %even_kernel.5 = (bf16[512,512]{1,0:T(8,128)(2,1)S(1)}, bf16[512,512]{1,0:T(8,128)(2,1)S(1)}) custom-call(bf16[512,512]{1,0:T(8,128)(2,1)S(1)} %get-tuple-element.89.refs_1_.x_ref, bf16[512,512]{1,0:T(8,128)(2,1)S(1)} %get-tuple-element.90.h_ref.refs_0_, bf16[512,512]{1,0:T(8,128)(2,1)S(1)} %get-tuple-element.74.adj_ref, ...), custom_call_target="tpu_custom_call" | custom-call | flops 134217728 | tf_op jit(solution)/shard_map/even_kernel/pallas_call | solution.py:464
  57.5 1.8 %odd_kernel.5 = (f32[512,512]{1,0:T(8,128)S(1)}, bf16[512,512]{1,0:T(8,128)(2,1)S(1)}, bf16[128,512]{1,0:T(8,128)(2,1)S(1)}, bf16[1024,512]{1,0:T(8,128)(2,1)S(1)}, bf16[128,512]{1,0:T(8,128)(2,1)S(1)}) custom-call(bf16[512,512]{1,0:T(8,128)(2,1)S(1)} %get-tuple-element.97.dep.x_ref, bf16[512,512]{1,0:T(8,128)(2,1)S(1)} %get-tuple-element.97.dep.x_ref, ...), custom_call_target="tpu_custom_call" | custom-call | flops 134217728 | tf_op jit(solution)/shard_map/odd_kernel/pallas_call | solution.py:474
  59.4 3.0 %collective-permute-done.17.recv_ref = bf16[128,512]{1,0:T(8,128)(2,1)S(1)} collective-permute-done((bf16[128,512]{1,0:T(8,128)(2,1)S(1)}, bf16[128,512]{1,0:T(8,128)(2,1)S(1)}, u32[]{:S(2)}, u32[]{:S(2)}) %collective-permute-start.17) | collective-permute-done | bytes 131104 | tf_op jit(solution)/shard_map/ppermute | solution.py:388
  65.5 1.8 %even_kernel.6 = (bf16[512,512]{1,0:T(8,128)(2,1)S(1)}, bf16[512,512]{1,0:T(8,128)(2,1)S(1)}) custom-call(bf16[512,512]{1,0:T(8,128)(2,1)S(1)} %get-tuple-element.103.x_ref, bf16[512,512]{1,0:T(8,128)(2,1)S(1)} %get-tuple-element.104.h_ref.refs_1_, bf16[512,512]{1,0:T(8,128)(2,1)S(1)} %get-tuple-element.74.adj_ref, ...), custom_call_target="tpu_custom_call" | custom-call | flops 134217728 | tf_op jit(solution)/shard_map/even_kernel/pallas_call | solution.py:464
  67.4 3.0 %collective-permute-start.23 = (bf16[528,512]{1,0:T(8,128)(2,1)S(1)}, bf16[528,512]{1,0:T(8,128)(2,1)S(1)}, u32[]{:S(2)}, u32[]{:S(2)}) collective-permute-start(bf16[528,512]{1,0:T(8,128)(2,1)S(1)} %select_kernel.10), channel_id=1, source_target_pairs={{24,0},{25,1},{26,2},{27,3},{28,4},{29,5},{30,6},{31,7},{16,8},{17... | collective-permute-start | bytes 1622024 | tf_op jit(solution)/shard_map/ppermute | solution.py:372
  70.4 1.7 %odd_kernel.6 = (f32[512,512]{1,0:T(8,128)S(1)}, bf16[512,512]{1,0:T(8,128)(2,1)S(1)}, bf16[128,512]{1,0:T(8,128)(2,1)S(1)}, bf16[1024,512]{1,0:T(8,128)(2,1)S(1)}, bf16[128,512]{1,0:T(8,128)(2,1)S(1)}) custom-call(bf16[512,512]{1,0:T(8,128)(2,1)S(1)} %get-tuple-element.111.dep.x_ref.refs_2_, bf16[512,512]{1,0:T(8,128)(2,1)S(1)} %get-tuple-element.111.dep.x_ref.refs_2_, ...), custom_call_target="tpu_custom_call" | custom-call | flops 5368709120 | tf_op jit(solution)/shard_map/odd_kernel/pallas_call | solution.py:474
  72.1 2.7 %collective-permute-done.20.recv_ref = bf16[128,512]{1,0:T(8,128)(2,1)S(1)} collective-permute-done((bf16[128,512]{1,0:T(8,128)(2,1)S(1)}, bf16[128,512]{1,0:T(8,128)(2,1)S(1)}, u32[]{:S(2)}, u32[]{:S(2)}) %collective-permute-start.20) | collective-permute-done | bytes 131104 | tf_op jit(solution)/shard_map/ppermute | solution.py:388
  78.1 1.8 %even_kernel.7 = (bf16[512,512]{1,0:T(8,128)(2,1)S(1)}, bf16[512,512]{1,0:T(8,128)(2,1)S(1)}) custom-call(bf16[512,512]{1,0:T(8,128)(2,1)S(1)} %get-tuple-element.117.x_ref, bf16[512,512]{1,0:T(8,128)(2,1)S(1)} %get-tuple-element.118.h_ref.refs_2_.refs_0_, bf16[512,512]{1,0:T(8,128)(2,1)S(1)} %get-tuple-element.74.adj_ref, ...), custom_call_target="tpu_custom_call" | custom-call | flops 134217728 | tf_op jit(solution)/shard_map/even_kernel/pallas_call | solution.py:464
  80.7 1.6 %collective-permute-done.23.dep.first_ref = bf16[528,512]{1,0:T(8,128)(2,1)S(1)} collective-permute-done((bf16[528,512]{1,0:T(8,128)(2,1)S(1)}, bf16[528,512]{1,0:T(8,128)(2,1)S(1)}, u32[]{:S(2)}, u32[]{:S(2)}) %collective-permute-start.23) | collective-permute-done | bytes 540704 | tf_op jit(solution)/shard_map/ppermute | solution.py:372
  82.2 1.4 %odd_kernel.7 = (f32[512,512]{1,0:T(8,128)S(1)}, bf16[512,512]{1,0:T(8,128)(2,1)S(1)}, bf16[128,512]{1,0:T(8,128)(2,1)S(1)}) custom-call(bf16[528,512]{1,0:T(8,128)(2,1)S(1)} %collective-permute-done.23.dep.first_ref, bf16[512,512]{1,0:T(8,128)(2,1)S(1)} %get-tuple-element.125.x_ref.refs_1_, bf16[512,512]{1,0:T(8,128)(2,1)S(1)} %get-tuple-element.74.adj_ref, ...), custom_call_target="tpu_custom_call" | custom-call | flops 5368709120 | tf_op jit(solution)/shard_map/odd_kernel/pallas_call | solution.py:474
  83.6 3.5 %collective-permute-done.22.recv_ref = bf16[128,512]{1,0:T(8,128)(2,1)S(1)} collective-permute-done((bf16[128,512]{1,0:T(8,128)(2,1)S(1)}, bf16[128,512]{1,0:T(8,128)(2,1)S(1)}, u32[]{:S(2)}, u32[]{:S(2)}) %collective-permute-start.22) | collective-permute-done | bytes 131104 | tf_op jit(solution)/shard_map/ppermute | solution.py:388
  89.3 3.0 %collective-permute-start.25 = (bf16[544,512]{1,0:T(8,128)(2,1)S(1)}, bf16[544,512]{1,0:T(8,128)(2,1)S(1)}, u32[]{:S(2)}, u32[]{:S(2)}) collective-permute-start(bf16[544,512]{1,0:T(8,128)(2,1)S(1)} %get-tuple-element.131), channel_id=1, source_target_pairs={{0,16},{1,17},{2,18},{3,19},{4,20},{5,21},{6,22},{7,23},{8,24},{9,... | collective-permute-start | bytes 1671176 | tf_op jit(solution)/shard_map/ppermute | solution.py:372
  93.0 1.3 %collective-permute-start.28 = (bf16[512,512]{1,0:T(8,128)(2,1)S(1)}, bf16[512,512]{1,0:T(8,128)(2,1)S(1)}, u32[]{:S(2)}, u32[]{:S(2)}) collective-permute-start(bf16[512,512]{1,0:T(8,128)(2,1)S(1)} %tie.11), channel_id=1, source_target_pairs={{8,24},{17,25},{10,26},{19,27},{12,28},{21,29},{14,30},{23,31}} | collective-permute-start | bytes 1572872 | tf_op jit(solution)/shard_map/ppermute | solution.py:511
  95.1 7.5 %collective-permute-done.24.one_ref = bf16[544,512]{1,0:T(8,128)(2,1)S(1)} collective-permute-done((bf16[544,512]{1,0:T(8,128)(2,1)S(1)}, bf16[544,512]{1,0:T(8,128)(2,1)S(1)}, u32[]{:S(2)}, u32[]{:S(2)}) %collective-permute-start.24) | collective-permute-done | bytes 557088 | tf_op jit(solution)/shard_map/ppermute | solution.py:372
  102.7 1.5 %collective-permute-done.25.two_ref = bf16[544,512]{1,0:T(8,128)(2,1)S(1)} collective-permute-done((bf16[544,512]{1,0:T(8,128)(2,1)S(1)}, bf16[544,512]{1,0:T(8,128)(2,1)S(1)}, u32[]{:S(2)}, u32[]{:S(2)}) %collective-permute-start.25) | collective-permute-done | bytes 557088 | tf_op jit(solution)/shard_map/ppermute | solution.py:372
  104.1 8.4 %collective-permute-done.28.three_ref = bf16[512,512]{1,0:T(8,128)(2,1)S(1)} collective-permute-done((bf16[512,512]{1,0:T(8,128)(2,1)S(1)}, bf16[512,512]{1,0:T(8,128)(2,1)S(1)}, u32[]{:S(2)}, u32[]{:S(2)}) %collective-permute-start.28) | collective-permute-done | bytes 524320 | tf_op jit(solution)/shard_map/ppermute | solution.py:511
  (89 shorter events, 24.0 us)
Async XLA Ops:
  1.4 11.6 %copy-start.8 = (s32[2,128]{1,0:T(2,128)S(1)}, s32[2,128]{1,0:T(2,128)}, u32[]{:S(2)}) copy-start(s32[2,128]{1,0:T(2,128)} %param.17) | copy-start | bytes 3076
  1.4 11.5 %copy-start.6 = (f32[2,512]{1,0:T(2,128)S(1)}, f32[2,512]{1,0:T(2,128)}, u32[]{:S(2)}) copy-start(f32[2,512]{1,0:T(2,128)} %param.12) | copy-start | bytes 12292
  1.6 10.7 %collective-permute-start.1 = (bf16[640,512]{1,0:T(8,128)(2,1)S(1)}, bf16[640,512]{1,0:T(8,128)(2,1)S(1)}, u32[]{:S(2)}, u32[]{:S(2)}) collective-permute-start(bf16[640,512]{1,0:T(8,128)(2,1)S(1)} %get-tuple-element.70.refs_1_.refs_0_), channel_id=1, source_target_pairs={{0,8},{1,17},{2,10},{3,19},{4,12},{5,21},{6,14},{7,23},{8,0},{9,25... | collective-permute-start | bytes 1966088 | tf_op jit(solution)/shard_map/ppermute | solution.py:372
  2.2 23.3 %collective-permute-start = (bf16[640,512]{1,0:T(8,128)(2,1)S(1)}, bf16[640,512]{1,0:T(8,128)(2,1)S(1)}, u32[]{:S(2)}, u32[]{:S(2)}) collective-permute-start(bf16[640,512]{1,0:T(8,128)(2,1)S(1)} %get-tuple-element.69.refs_1_.refs_0_), channel_id=1, source_target_pairs={{0,8},{1,17},{2,10},{3,19},{4,12},{5,21},{6,14},{7,23},{8,0},{9,25... | collective-permute-start | bytes 1966088 | tf_op jit(solution)/shard_map/ppermute | solution.py:372
  12.3 14.7 %collective-permute-start.6 = (bf16[640,512]{1,0:T(8,128)(2,1)S(1)}, bf16[640,512]{1,0:T(8,128)(2,1)S(1)}, u32[]{:S(2)}, u32[]{:S(2)}) collective-permute-start(bf16[640,512]{1,0:T(8,128)(2,1)S(1)} %select_kernel.6.refs_2_), channel_id=1, source_target_pairs={{0,16},{1,9},{2,18},{3,11},{4,20},{5,13},{6,22},{7,15},{8,24},{9,1... | collective-permute-start | bytes 1966088 | tf_op jit(solution)/shard_map/ppermute | solution.py:372
  12.9 11.8 %collective-permute-start.4 = (f32[2,1152]{1,0:T(2,128)S(1)}, f32[2,1152]{1,0:T(2,128)S(1)}, u32[]{:S(2)}, u32[]{:S(2)}) collective-permute-start(f32[2,1152]{1,0:T(2,128)S(1)} %tie.6.s0), channel_id=1, source_target_pairs={{0,24},{1,25},{2,26},{3,27},{4,28},{5,29},{6,30},{7,31},{8,16},{9,... | collective-permute-start | bytes 27656 | tf_op jit(solution)/shard_map/ppermute | solution.py:372
  14.5 11.0 %collective-permute-start.3 = (f32[2,1152]{1,0:T(2,128)S(1)}, f32[2,1152]{1,0:T(2,128)S(1)}, u32[]{:S(2)}, u32[]{:S(2)}) collective-permute-start(f32[2,1152]{1,0:T(2,128)S(1)} %tie.6.s0), channel_id=1, source_target_pairs={{0,16},{1,17},{2,18},{3,19},{4,20},{5,21},{6,22},{7,23},{8,24},{9,... | collective-permute-start | bytes 27656 | tf_op jit(solution)/shard_map/ppermute | solution.py:372
  14.6 10.9 %collective-permute-start.2 = (f32[2,1152]{1,0:T(2,128)S(1)}, f32[2,1152]{1,0:T(2,128)S(1)}, u32[]{:S(2)}, u32[]{:S(2)}) collective-permute-start(f32[2,1152]{1,0:T(2,128)S(1)} %tie.6.s0), channel_id=1, source_target_pairs={{0,8},{1,9},{2,10},{3,11},{4,12},{5,13},{6,14},{7,15},{8,0},{9,1},... | collective-permute-start | bytes 27656 | tf_op jit(solution)/shard_map/ppermute | solution.py:372
  25.6 10.7 %collective-permute-start.11 = (bf16[640,512]{1,0:T(8,128)(2,1)S(1)}, bf16[640,512]{1,0:T(8,128)(2,1)S(1)}, u32[]{:S(2)}, u32[]{:S(2)}) collective-permute-start(bf16[640,512]{1,0:T(8,128)(2,1)S(1)} %select_kernel.7.dep.refs_2_), channel_id=1, source_target_pairs={{0,16},{1,9},{2,18},{3,11},{4,20},{5,13},{6,22},{7,15},{8,24},{9,1... | collective-permute-start | bytes 1966088 | tf_op jit(solution)/shard_map/ppermute | solution.py:372
  26.5 5.2 %collective-permute-start.7 = (bf16[512,512]{1,0:T(8,128)(2,1)S(1)}, bf16[512,512]{1,0:T(8,128)(2,1)S(1)}, u32[]{:S(2)}, u32[]{:S(2)}) collective-permute-start(bf16[512,512]{1,0:T(8,128)(2,1)S(1)} %top_kernel.2), channel_id=1, source_target_pairs={{0,1},{1,0},{2,3},{3,2},{4,5},{5,4},{6,7},{7,6},{8,9},{9,8},{10,11... | collective-permute-start | bytes 1572872 | tf_op jit(solution)/shard_map/ppermute | solution.py:372
  27.1 4.6 %collective-permute-start.8 = (bf16[512,512]{1,0:T(8,128)(2,1)S(1)}, bf16[512,512]{1,0:T(8,128)(2,1)S(1)}, u32[]{:S(2)}, u32[]{:S(2)}) collective-permute-start(bf16[512,512]{1,0:T(8,128)(2,1)S(1)} %top_kernel.3), channel_id=1, source_target_pairs={{0,1},{1,0},{2,3},{3,2},{4,5},{5,4},{6,7},{7,6},{8,9},{9,8},{10,11... | collective-permute-start | bytes 1572872 | tf_op jit(solution)/shard_map/ppermute | solution.py:372
  29.0 3.7 %collective-permute-start.5 = (bf16[128,512]{1,0:T(8,128)(2,1)S(1)}, bf16[128,512]{1,0:T(8,128)(2,1)S(1)}, u32[]{:S(2)}, u32[]{:S(2)}) collective-permute-start(bf16[128,512]{1,0:T(8,128)(2,1)S(1)} %get-tuple-element.71), channel_id=1, source_target_pairs={{0,1},{1,0},{2,3},{3,2},{4,5},{5,4},{6,7},{7,6},{8,9},{9,8},{10,11... | collective-permute-start | bytes 393224 | tf_op jit(solution)/shard_map/ppermute | solution.py:388
  30.2 13.1 %collective-permute-start.10 = (bf16[640,512]{1,0:T(8,128)(2,1)S(1)}, bf16[640,512]{1,0:T(8,128)(2,1)S(1)}, u32[]{:S(2)}, u32[]{:S(2)}) collective-permute-start(bf16[640,512]{1,0:T(8,128)(2,1)S(1)} %select_kernel.8.refs_2_), channel_id=1, source_target_pairs={{0,16},{1,9},{2,18},{3,11},{4,20},{5,13},{6,22},{7,15},{8,24},{9,1... | collective-permute-start | bytes 1966088 | tf_op jit(solution)/shard_map/ppermute | solution.py:372
  33.3 10.0 %collective-permute-start.12 = (bf16[640,512]{1,0:T(8,128)(2,1)S(1)}, bf16[640,512]{1,0:T(8,128)(2,1)S(1)}, u32[]{:S(2)}, u32[]{:S(2)}) collective-permute-start(bf16[640,512]{1,0:T(8,128)(2,1)S(1)} %tie.7.refs_2_), channel_id=1, source_target_pairs={{0,1},{1,0},{2,3},{3,2},{4,5},{5,4},{6,7},{7,6},{8,9},{9,8},{10,11... | collective-permute-start | bytes 1966088 | tf_op jit(solution)/shard_map/ppermute | solution.py:372
  36.2 7.0 %collective-permute-start.13 = (bf16[640,512]{1,0:T(8,128)(2,1)S(1)}, bf16[640,512]{1,0:T(8,128)(2,1)S(1)}, u32[]{:S(2)}, u32[]{:S(2)}) collective-permute-start(bf16[640,512]{1,0:T(8,128)(2,1)S(1)} %tie.8.refs_3_), channel_id=1, source_target_pairs={{0,1},{1,0},{2,3},{3,2},{4,5},{5,4},{6,7},{7,6},{8,9},{9,8},{10,11... | collective-permute-start | bytes 1966088 | tf_op jit(solution)/shard_map/ppermute | solution.py:372
  36.4 13.8 %collective-permute-start.15 = (bf16[640,512]{1,0:T(8,128)(2,1)S(1)}, bf16[640,512]{1,0:T(8,128)(2,1)S(1)}, u32[]{:S(2)}, u32[]{:S(2)}) collective-permute-start(bf16[640,512]{1,0:T(8,128)(2,1)S(1)} %select_kernel.9.dep), channel_id=1, source_target_pairs={{0,16},{1,9},{2,18},{3,11},{4,20},{5,13},{6,22},{7,15},{8,24},{9,1... | collective-permute-start | bytes 1966088 | tf_op jit(solution)/shard_map/ppermute | solution.py:372
  37.8 8.3 %collective-permute-start.9 = (bf16[128,512]{1,0:T(8,128)(2,1)S(1)}, bf16[128,512]{1,0:T(8,128)(2,1)S(1)}, u32[]{:S(2)}, u32[]{:S(2)}) collective-permute-start(bf16[128,512]{1,0:T(8,128)(2,1)S(1)} %send_kernel.4.dep.refs_1_), channel_id=1, source_target_pairs={{0,4},{1,5},{2,6},{3,7},{4,0},{5,1},{6,2},{7,3},{8,12},{9,13},{10,... | collective-permute-start | bytes 393224 | tf_op jit(solution)/shard_map/ppermute | solution.py:388
  46.1 4.7 %collective-permute-start.16 = (bf16[640,512]{1,0:T(8,128)(2,1)S(1)}, bf16[640,512]{1,0:T(8,128)(2,1)S(1)}, u32[]{:S(2)}, u32[]{:S(2)}) collective-permute-start(bf16[640,512]{1,0:T(8,128)(2,1)S(1)} %tie.10.refs_4_.refs_12_), channel_id=1, source_target_pairs={{0,1},{1,0},{2,3},{3,2},{4,5},{5,4},{6,7},{7,6},{8,9},{9,8},{10,11... | collective-permute-start | bytes 1966088 | tf_op jit(solution)/shard_map/ppermute | solution.py:372
  50.3 7.3 %collective-permute-start.18 = (bf16[640,512]{1,0:T(8,128)(2,1)S(1)}, bf16[640,512]{1,0:T(8,128)(2,1)S(1)}, u32[]{:S(2)}, u32[]{:S(2)}) collective-permute-start(bf16[640,512]{1,0:T(8,128)(2,1)S(1)} %tie.9.dep.refs_4_), channel_id=1, source_target_pairs={{0,1},{1,0},{2,3},{3,2},{4,5},{5,4},{6,7},{7,6},{8,9},{9,8},{10,11... | collective-permute-start | bytes 1966088 | tf_op jit(solution)/shard_map/ppermute | solution.py:372
  50.4 2.2 %collective-permute-start.14 = (bf16[128,512]{1,0:T(8,128)(2,1)S(1)}, bf16[128,512]{1,0:T(8,128)(2,1)S(1)}, u32[]{:S(2)}, u32[]{:S(2)}) collective-permute-start(bf16[128,512]{1,0:T(8,128)(2,1)S(1)} %get-tuple-element.88), channel_id=1, source_target_pairs={{0,1},{1,0},{2,3},{3,2},{4,5},{5,4},{6,7},{7,6},{8,9},{9,8},{10,11... | collective-permute-start | bytes 393224 | tf_op jit(solution)/shard_map/ppermute | solution.py:388
  53.1 9.3 %collective-permute-start.17 = (bf16[128,512]{1,0:T(8,128)(2,1)S(1)}, bf16[128,512]{1,0:T(8,128)(2,1)S(1)}, u32[]{:S(2)}, u32[]{:S(2)}) collective-permute-start(bf16[128,512]{1,0:T(8,128)(2,1)S(1)} %send_kernel.5.dep), channel_id=1, source_target_pairs={{0,4},{1,5},{2,6},{3,7},{4,0},{5,1},{6,2},{7,3},{8,12},{9,13},{10,... | collective-permute-start | bytes 393224 | tf_op jit(solution)/shard_map/ppermute | solution.py:388
  63.5 1.4 %collective-permute-start.19 = (bf16[128,512]{1,0:T(8,128)(2,1)S(1)}, bf16[128,512]{1,0:T(8,128)(2,1)S(1)}, u32[]{:S(2)}, u32[]{:S(2)}) collective-permute-start(bf16[128,512]{1,0:T(8,128)(2,1)S(1)} %get-tuple-element.102), channel_id=1, source_target_pairs={{0,1},{1,0},{2,3},{3,2},{4,5},{5,4},{6,7},{7,6},{8,9},{9,8},{10,11... | collective-permute-start | bytes 393224 | tf_op jit(solution)/shard_map/ppermute | solution.py:388
  65.5 9.3 %collective-permute-start.20 = (bf16[128,512]{1,0:T(8,128)(2,1)S(1)}, bf16[128,512]{1,0:T(8,128)(2,1)S(1)}, u32[]{:S(2)}, u32[]{:S(2)}) collective-permute-start(bf16[128,512]{1,0:T(8,128)(2,1)S(1)} %send_kernel.6.dep), channel_id=1, source_target_pairs={{0,4},{1,5},{2,6},{3,7},{4,0},{5,1},{6,2},{7,3},{8,12},{9,13},{10,... | collective-permute-start | bytes 393224 | tf_op jit(solution)/shard_map/ppermute | solution.py:388
  67.4 14.8 %collective-permute-start.23 = (bf16[528,512]{1,0:T(8,128)(2,1)S(1)}, bf16[528,512]{1,0:T(8,128)(2,1)S(1)}, u32[]{:S(2)}, u32[]{:S(2)}) collective-permute-start(bf16[528,512]{1,0:T(8,128)(2,1)S(1)} %select_kernel.10), channel_id=1, source_target_pairs={{24,0},{25,1},{26,2},{27,3},{28,4},{29,5},{30,6},{31,7},{16,8},{17... | collective-permute-start | bytes 1622024 | tf_op jit(solution)/shard_map/ppermute | solution.py:372
  75.9 1.4 %collective-permute-start.21 = (bf16[128,512]{1,0:T(8,128)(2,1)S(1)}, bf16[128,512]{1,0:T(8,128)(2,1)S(1)}, u32[]{:S(2)}, u32[]{:S(2)}) collective-permute-start(bf16[128,512]{1,0:T(8,128)(2,1)S(1)} %get-tuple-element.116), channel_id=1, source_target_pairs={{0,1},{1,0},{2,3},{3,2},{4,5},{5,4},{6,7},{7,6},{8,9},{9,8},{10,11... | collective-permute-start | bytes 393224 | tf_op jit(solution)/shard_map/ppermute | solution.py:388
  77.8 9.3 %collective-permute-start.22 = (bf16[128,512]{1,0:T(8,128)(2,1)S(1)}, bf16[128,512]{1,0:T(8,128)(2,1)S(1)}, u32[]{:S(2)}, u32[]{:S(2)}) collective-permute-start(bf16[128,512]{1,0:T(8,128)(2,1)S(1)} %send_kernel.7.dep), channel_id=1, source_target_pairs={{0,4},{1,5},{2,6},{3,7},{4,0},{5,1},{6,2},{7,3},{8,12},{9,13},{10,... | collective-permute-start | bytes 393224 | tf_op jit(solution)/shard_map/ppermute | solution.py:388
  80.0 12.3 %collective-permute-start.27 = (bf16[528,512]{1,0:T(8,128)(2,1)S(1)}, bf16[528,512]{1,0:T(8,128)(2,1)S(1)}, u32[]{:S(2)}, u32[]{:S(2)}) collective-permute-start(bf16[528,512]{1,0:T(8,128)(2,1)S(1)} %select_kernel.11), channel_id=1, source_target_pairs={{8,16},{9,25},{10,18},{11,27},{12,20},{13,29},{14,22},{15,31}} | collective-permute-start | bytes 1622024 | tf_op jit(solution)/shard_map/ppermute | solution.py:372
  88.0 5.0 %collective-permute-start.26 = (bf16[512,512]{1,0:T(8,128)(2,1)S(1)}, bf16[512,512]{1,0:T(8,128)(2,1)S(1)}, u32[]{:S(2)}, u32[]{:S(2)}) collective-permute-start(bf16[512,512]{1,0:T(8,128)(2,1)S(1)} %get-tuple-element.132.refs_3_), channel_id=1, source_target_pairs={{0,8},{1,17},{2,10},{3,19},{4,12},{5,21},{6,14},{7,23}} | collective-permute-start | bytes 1572872 | tf_op jit(solution)/shard_map/ppermute | solution.py:372
  88.7 13.9 %collective-permute-start.24 = (bf16[544,512]{1,0:T(8,128)(2,1)S(1)}, bf16[544,512]{1,0:T(8,128)(2,1)S(1)}, u32[]{:S(2)}, u32[]{:S(2)}) collective-permute-start(bf16[544,512]{1,0:T(8,128)(2,1)S(1)} %get-tuple-element.130), channel_id=1, source_target_pairs={{0,8},{1,9},{2,10},{3,11},{4,12},{5,13},{6,14},{7,15},{8,0},{9,1},... | collective-permute-start | bytes 1671176 | tf_op jit(solution)/shard_map/ppermute | solution.py:372
  89.3 14.8 %collective-permute-start.25 = (bf16[544,512]{1,0:T(8,128)(2,1)S(1)}, bf16[544,512]{1,0:T(8,128)(2,1)S(1)}, u32[]{:S(2)}, u32[]{:S(2)}) collective-permute-start(bf16[544,512]{1,0:T(8,128)(2,1)S(1)} %get-tuple-element.131), channel_id=1, source_target_pairs={{0,16},{1,17},{2,18},{3,19},{4,20},{5,21},{6,22},{7,23},{8,24},{9,... | collective-permute-start | bytes 1671176 | tf_op jit(solution)/shard_map/ppermute | solution.py:372
  92.3 11.8 %collective-permute-start.29 = (bf16[528,512]{1,0:T(8,128)(2,1)S(1)}, bf16[528,512]{1,0:T(8,128)(2,1)S(1)}, u32[]{:S(2)}, u32[]{:S(2)}) collective-permute-start(bf16[528,512]{1,0:T(8,128)(2,1)S(1)} %collective-permute-done.27.refs_1_.early_ref), channel_id=1, source_target_pairs={{25,17},{27,19},{29,21},{31,23}} | collective-permute-start | bytes 1622024 | tf_op jit(solution)/shard_map/ppermute | solution.py:511
  93.0 19.5 %collective-permute-start.28 = (bf16[512,512]{1,0:T(8,128)(2,1)S(1)}, bf16[512,512]{1,0:T(8,128)(2,1)S(1)}, u32[]{:S(2)}, u32[]{:S(2)}) collective-permute-start(bf16[512,512]{1,0:T(8,128)(2,1)S(1)} %tie.11), channel_id=1, source_target_pairs={{8,24},{17,25},{10,26},{19,27},{12,28},{21,29},{14,30},{23,31}} | collective-permute-start | bytes 1572872 | tf_op jit(solution)/shard_map/ppermute | solution.py:511
  (7 other events, 22.2 us)
where the time goes:
time: 114 us
  waiting for transfers between devices  55.9 us (49%)
  starting transfers between devices  28.2 us (25%)
  Pallas kernels  27.6 us (24%)
  local copies, waits for them, and re-layouts  1.4 us (1%)
    ppermute x20, waiting for transfers between devices, moved(): return lax.ppermute(value, ('segment', 'dom'), pairs)  35.1 us
    ppermute x20, starting transfers between devices, moved(): return lax.ppermute(value, ('segment', 'dom'), pairs)  19 us
    ppermute x8, waiting for transfers between devices, exchange(): return lax.ppermute(sent, 'dom', [(i, i ^ 1 << bit) for i in range(doms)])  12.5 us
    ppermute x2, waiting for transfers between devices, onward(): return lax.ppermute(value, ('segment', 'dom'), pairs)  8.36 us
    ppermute x8, starting transfers between devices, exchange(): return lax.ppermute(sent, 'dom', [(i, i ^ 1 << bit) for i in range(doms)])  7.27 us
    pallas_call x4, Pallas kernels, shards(): call(functools.partial(even_kernel, k), (mat, mat), [VM] * 7 + [ANY], flo...  7.15 us
    pallas_call x4, Pallas kernels, shards(): call(functools.partial(odd_kernel, k, fetch), (mat32, half, edge) + ((bot...  6.23 us
    pallas_call x4, Pallas kernels, shards(): call(functools.partial(finish_kernel, k, last), (mat, tall, tall) if last...  4.24 us
  transfers between devices with their start and end apart: 30, of which 17 were waited for; matrix products, arithmetic and copies ran while one was open for 0% of the time, Pallas kernels for 22%

commit v1 on v0

--- a/solution.py
+++ b/solution.py
@@ -448,8 +448,7 @@
         if k > 0:
             recv = exchange(sent, 0)
         if k == 1:
-            c1 = tie(c1, x)
-            w, c = loaded(1, c1)
+            w, c = loaded(1, x)
         edges = call(
             functools.partial(edge_kernel, k),
             (edge32, edge32, jax.ShapeDtypeStruct((bound, bound), BF16), edge),
@@ -459,7 +458,7 @@
         sent = call(functools.partial(send_kernel, k), edge, [VM] * 7, flops=LOAD * unit / 4)(recv, *edges[:3], edges[3], w, small)
         recv2 = exchange(sent, 1)
         if k == 1:
-            brought[1].append(c1)
+            brought[1].append(tie(c1, sent))
             swapped[1].append(moved(brought[1][2], sibling))
         h, x = call(functools.partial(even_kernel, k), (mat, mat), [VM] * 7 + [ANY], flops=LOAD * unit)(
             x, h, adj, recv, w, c, small, sent
@@ -480,7 +479,7 @@
         )(c0 if k == 0 else first_two if last else x, x, adj, small, *cands, *ahead)
         if k == 0:
             brought[0].append(tie(c0, recv2, z))
-            swapped[0].append(moved(brought[0][2], sibling))
+            swapped[0].append(moved(call(top_kernel, half, [ANY, VM])(z, brought[0][2]), sibling))
         if k == 2:
             (pay,) = select(ends, [[(j ^ 3,) for j in range(2)]], [x], extra=16)
             first_two = moved(pay, across(3), [j ^ 3 for j in range(2)])

time: 114 us -> 112 us (0.982)
  waiting for transfers between devices: 55.9 us -> 54.2 us
    ppermute x20, waiting for transfers between devices: 35.1 us -> 33.4 us  [moved(): return lax.ppermute(value, ('segment', 'dom'), pairs)]
where the time goes in v1:
time: 112 us; the launch traced here: 111 us
  waiting for transfers between devices  54.2 us (48%)
  Pallas kernels  27.6 us (25%)
  starting transfers between devices  27.4 us (24%)
  local copies, waits for them, and re-layouts  1.4 us (1%)
    ppermute x20, waiting for transfers between devices, moved(): return lax.ppermute(value, ('segment', 'dom'), pairs)  33.4 us
    ppermute x20, starting transfers between devices, moved(): return lax.ppermute(value, ('segment', 'dom'), pairs)  18.3 us
    ppermute x8, waiting for transfers between devices, exchange(): return lax.ppermute(sent, 'dom', [(i, i ^ 1 << bit) for i in range(doms)])  12.5 us
    ppermute x2, waiting for transfers between devices, onward(): return lax.ppermute(value, ('segment', 'dom'), pairs)  8.36 us
    ppermute x8, starting transfers between devices, exchange(): return lax.ppermute(sent, 'dom', [(i, i ^ 1 << bit) for i in range(doms)])  7.15 us
    pallas_call x4, Pallas kernels, shards(): call(functools.partial(even_kernel, k), (mat, mat), [VM] * 7 + [ANY], flo...  7.12 us
    pallas_call x4, Pallas kernels, shards(): call(functools.partial(odd_kernel, k, fetch), (mat32, half, edge) + ((bot...  6.24 us
    pallas_call x4, Pallas kernels, shards(): call(functools.partial(finish_kernel, k, last), (mat, tall, tall) if last...  4.26 us
  transfers between devices with their start and end apart: 30, of which 17 were waited for; matrix products, arithmetic and copies ran while one was open for 0% of the time, Pallas kernels for 22%

profile of v1, /device:TPU:6, one launch (start us, length us, event | category | flops | bytes accessed | tf_op | source)
XLA Modules:
  0.0 111.3 jit_solution(1820166871942502056)
XLA Ops:
  0.0 1.3 %constant_dynamic-slice_fusion.own = bf16[2,512,512]{2,1,0:T(8,128)(2,1)S(1)} fusion(bf16[2,1024,512]{2,1,0:T(8,128)(2,1)} %refs_0_.11, s32[]{:T(128)S(6)} %select_n.3), kind=kLoop, calls=%fused_computation.1 | loop fusion | bytes 2097156 | tf_op jit(solution)/shard_map/dynamic_slice | solution.py:407
  2.2 1.5 %collective-permute-start = (bf16[640,512]{1,0:T(8,128)(2,1)S(1)}, bf16[640,512]{1,0:T(8,128)(2,1)S(1)}, u32[]{:S(2)}, u32[]{:S(2)}) collective-permute-start(bf16[640,512]{1,0:T(8,128)(2,1)S(1)} %get-tuple-element.69.refs_1_.refs_0_), channel_id=1, source_target_pairs={{0,8},{1,17},{2,10},{3,19},{4,12},{5,21},{6,14},{7,23},{8,0},{9,25... | collective-permute-start | bytes 1966088 | tf_op jit(solution)/shard_map/ppermute | solution.py:372
  3.7 8.6 %collective-permute-done.1.refs_0_.refs_1_.in_ref.refs_2_.refs_10_ = bf16[640,512]{1,0:T(8,128)(2,1)S(1)} collective-permute-done((bf16[640,512]{1,0:T(8,128)(2,1)S(1)}, bf16[640,512]{1,0:T(8,128)(2,1)S(1)}, u32[]{:S(2)}, u32[]{:S(2)}) %collective-permute-start.1) | collective-permute-done | bytes 655392 | tf_op jit(solution)/shard_map/ppermute | solution.py:372
  12.9 1.6 %collective-permute-start.4 = (f32[2,1152]{1,0:T(2,128)S(1)}, f32[2,1152]{1,0:T(2,128)S(1)}, u32[]{:S(2)}, u32[]{:S(2)}) collective-permute-start(f32[2,1152]{1,0:T(2,128)S(1)} %tie.6.s0), channel_id=1, source_target_pairs={{0,24},{1,25},{2,26},{3,27},{4,28},{5,29},{6,30},{7,31},{8,16},{9,... | collective-permute-start | bytes 27656 | tf_op jit(solution)/shard_map/ppermute | solution.py:372
  14.6 1.9 %collective-permute-start.2 = (f32[2,1152]{1,0:T(2,128)S(1)}, f32[2,1152]{1,0:T(2,128)S(1)}, u32[]{:S(2)}, u32[]{:S(2)}) collective-permute-start(f32[2,1152]{1,0:T(2,128)S(1)} %tie.6.s0), channel_id=1, source_target_pairs={{0,8},{1,9},{2,10},{3,11},{4,12},{5,13},{6,14},{7,15},{8,0},{9,1},... | collective-permute-start | bytes 27656 | tf_op jit(solution)/shard_map/ppermute | solution.py:372
  16.5 8.2 %collective-permute-done.4.refs_5_.s3 = f32[2,1152]{1,0:T(2,128)S(1)} collective-permute-done((f32[2,1152]{1,0:T(2,128)S(1)}, f32[2,1152]{1,0:T(2,128)S(1)}, u32[]{:S(2)}, u32[]{:S(2)}) %collective-permute-start.4) | collective-permute-done | bytes 9248 | tf_op jit(solution)/shard_map/ppermute | solution.py:372
  27.2 1.8 %first_kernel.1 = (bf16[512,512]{1,0:T(8,128)(2,1)S(1)}, bf16[512,512]{1,0:T(8,128)(2,1)S(1)}, bf16[512,512]{1,0:T(8,128)(2,1)S(1)}, bf16[128,512]{1,0:T(8,128)(...) custom-call(bf16[640,512]{1,0:T(8,128)(2,1)S(1)} %select_kernel.7.dep.refs_2_, ...), custom_call_target="tpu_custom_call" | custom-call | tf_op jit(solution)/shard_map/first_kernel/pallas_call | solution.py:421
  30.2 1.5 %collective-permute-start.10 = (bf16[640,512]{1,0:T(8,128)(2,1)S(1)}, bf16[640,512]{1,0:T(8,128)(2,1)S(1)}, u32[]{:S(2)}, u32[]{:S(2)}) collective-permute-start(bf16[640,512]{1,0:T(8,128)(2,1)S(1)} %select_kernel.8.refs_2_), channel_id=1, source_target_pairs={{0,16},{1,9},{2,18},{3,11},{4,20},{5,13},{6,22},{7,15},{8,24},{9,1... | collective-permute-start | bytes 1966088 | tf_op jit(solution)/shard_map/ppermute | solution.py:372
  33.4 2.9 %collective-permute-done.11.refs_0_ = bf16[640,512]{1,0:T(8,128)(2,1)S(1)} collective-permute-done((bf16[640,512]{1,0:T(8,128)(2,1)S(1)}, bf16[640,512]{1,0:T(8,128)(2,1)S(1)}, u32[]{:S(2)}, u32[]{:S(2)}) %collective-permute-start.11) | collective-permute-done | bytes 655392 | tf_op jit(solution)/shard_map/ppermute | solution.py:372
  36.4 2.6 %collective-permute-start.9 = (bf16[128,512]{1,0:T(8,128)(2,1)S(1)}, bf16[128,512]{1,0:T(8,128)(2,1)S(1)}, u32[]{:S(2)}, u32[]{:S(2)}) collective-permute-start(bf16[128,512]{1,0:T(8,128)(2,1)S(1)} %send_kernel.4.dep.refs_1_), channel_id=1, source_target_pairs={{0,4},{1,5},{2,6},{3,7},{4,0},{5,1},{6,2},{7,3},{8,12},{9,13},{10,... | collective-permute-start | bytes 393224 | tf_op jit(solution)/shard_map/ppermute | solution.py:388
  39.0 1.4 %collective-permute-start.17 = (bf16[640,512]{1,0:T(8,128)(2,1)S(1)}, bf16[640,512]{1,0:T(8,128)(2,1)S(1)}, u32[]{:S(2)}, u32[]{:S(2)}) collective-permute-start(bf16[640,512]{1,0:T(8,128)(2,1)S(1)} %select_kernel.9.dep), channel_id=1, source_target_pairs={{0,16},{1,9},{2,18},{3,11},{4,20},{5,13},{6,22},{7,15},{8,24},{9,1... | collective-permute-start | bytes 1966088 | tf_op jit(solution)/shard_map/ppermute | solution.py:372
  40.4 1.8 %even_kernel.4 = (bf16[512,512]{1,0:T(8,128)(2,1)S(1)}, bf16[512,512]{1,0:T(8,128)(2,1)S(1)}) custom-call(bf16[512,512]{1,0:T(8,128)(2,1)S(1)} %get-tuple-element.72.x_ref, bf16[512,512]{1,0:T(8,128)(2,1)S(1)} %get-tuple-element.73.h_ref, bf16[512,512]{1,0:T(8,128)(2,1)S(1)} %get-tuple-element.74.adj_ref, ...), custom_call_target="tpu_custom_call" | custom-call | flops 134217728 | tf_op jit(solution)/shard_map/even_kernel/pallas_call | solution.py:463
  43.3 1.3 %odd_kernel.4 = (f32[512,512]{1,0:T(8,128)S(1)}, bf16[512,512]{1,0:T(8,128)(2,1)S(1)}, bf16[128,512]{1,0:T(8,128)(2,1)S(1)}) custom-call(bf16[640,512]{1,0:T(8,128)(2,1)S(1)} %collective-permute-done.10.dep.refs_0_, bf16[512,512]{1,0:T(8,128)(2,1)S(1)} %get-tuple-element.83.x_ref, bf16[512,512]{1,0:T(8,128)(2,1)S(1)} %get-tuple-element.74.adj_ref, ...), custom_call_target="tpu_custom_call" | custom-call | flops 134217728 | tf_op jit(solution)/shard_map/odd_kernel/pallas_call | solution.py:473
  44.6 1.2 %collective-permute-done.9.recv_ref.refs_1_ = bf16[128,512]{1,0:T(8,128)(2,1)S(1)} collective-permute-done((bf16[128,512]{1,0:T(8,128)(2,1)S(1)}, bf16[128,512]{1,0:T(8,128)(2,1)S(1)}, u32[]{:S(2)}, u32[]{:S(2)}) %collective-permute-start.9) | collective-permute-done | bytes 131104 | tf_op jit(solution)/shard_map/ppermute | solution.py:388
  50.4 2.6 %collective-permute-start.16 = (bf16[128,512]{1,0:T(8,128)(2,1)S(1)}, bf16[128,512]{1,0:T(8,128)(2,1)S(1)}, u32[]{:S(2)}, u32[]{:S(2)}) collective-permute-start(bf16[128,512]{1,0:T(8,128)(2,1)S(1)} %send_kernel.5.dep.refs_1_), channel_id=1, source_target_pairs={{0,4},{1,5},{2,6},{3,7},{4,0},{5,1},{6,2},{7,3},{8,12},{9,13},{10,... | collective-permute-start | bytes 393224 | tf_op jit(solution)/shard_map/ppermute | solution.py:388
  53.0 1.8 %even_kernel.5 = (bf16[512,512]{1,0:T(8,128)(2,1)S(1)}, bf16[512,512]{1,0:T(8,128)(2,1)S(1)}) custom-call(bf16[512,512]{1,0:T(8,128)(2,1)S(1)} %get-tuple-element.89.dep.x_ref, bf16[512,512]{1,0:T(8,128)(2,1)S(1)} %get-tuple-element.90.h_ref.refs_0_, bf16[512,512]{1,0:T(8,128)(2,1)S(1)} %get-tuple-element.74.adj_ref, ...), custom_call_target="tpu_custom_call" | custom-call | flops 134217728 | tf_op jit(solution)/shard_map/even_kernel/pallas_call | solution.py:463
  54.8 1.8 %odd_kernel.5 = (f32[512,512]{1,0:T(8,128)S(1)}, bf16[512,512]{1,0:T(8,128)(2,1)S(1)}, bf16[128,512]{1,0:T(8,128)(2,1)S(1)}, bf16[1024,512]{1,0:T(8,128)(2,1)S(1)}, bf16[128,512]{1,0:T(8,128)(2,1)S(1)}) custom-call(bf16[512,512]{1,0:T(8,128)(2,1)S(1)} %get-tuple-element.97.dep.x_ref, bf16[512,512]{1,0:T(8,128)(2,1)S(1)} %get-tuple-element.97.dep.x_ref, ...), custom_call_target="tpu_custom_call" | custom-call | flops 134217728 | tf_op jit(solution)/shard_map/odd_kernel/pallas_call | solution.py:473
  56.7 3.2 %collective-permute-done.16.recv_ref = bf16[128,512]{1,0:T(8,128)(2,1)S(1)} collective-permute-done((bf16[128,512]{1,0:T(8,128)(2,1)S(1)}, bf16[128,512]{1,0:T(8,128)(2,1)S(1)}, u32[]{:S(2)}, u32[]{:S(2)}) %collective-permute-start.16) | collective-permute-done | bytes 131104 | tf_op jit(solution)/shard_map/ppermute | solution.py:388
  63.0 1.8 %even_kernel.6 = (bf16[512,512]{1,0:T(8,128)(2,1)S(1)}, bf16[512,512]{1,0:T(8,128)(2,1)S(1)}) custom-call(bf16[512,512]{1,0:T(8,128)(2,1)S(1)} %get-tuple-element.103.x_ref, bf16[512,512]{1,0:T(8,128)(2,1)S(1)} %get-tuple-element.104.h_ref.refs_1_, bf16[512,512]{1,0:T(8,128)(2,1)S(1)} %get-tuple-element.74.adj_ref, ...), custom_call_target="tpu_custom_call" | custom-call | flops 134217728 | tf_op jit(solution)/shard_map/even_kernel/pallas_call | solution.py:463
  64.9 2.7 %collective-permute-start.23 = (bf16[528,512]{1,0:T(8,128)(2,1)S(1)}, bf16[528,512]{1,0:T(8,128)(2,1)S(1)}, u32[]{:S(2)}, u32[]{:S(2)}) collective-permute-start(bf16[528,512]{1,0:T(8,128)(2,1)S(1)} %select_kernel.10), channel_id=1, source_target_pairs={{24,0},{25,1},{26,2},{27,3},{28,4},{29,5},{30,6},{31,7},{16,8},{17... | collective-permute-start | bytes 1622024 | tf_op jit(solution)/shard_map/ppermute | solution.py:372
  67.6 1.7 %odd_kernel.6 = (f32[512,512]{1,0:T(8,128)S(1)}, bf16[512,512]{1,0:T(8,128)(2,1)S(1)}, bf16[128,512]{1,0:T(8,128)(2,1)S(1)}, bf16[1024,512]{1,0:T(8,128)(2,1)S(1)}, bf16[128,512]{1,0:T(8,128)(2,1)S(1)}) custom-call(bf16[512,512]{1,0:T(8,128)(2,1)S(1)} %get-tuple-element.111.dep.x_ref.refs_2_, bf16[512,512]{1,0:T(8,128)(2,1)S(1)} %get-tuple-element.111.dep.x_ref.refs_2_, ...), custom_call_target="tpu_custom_call" | custom-call | flops 5368709120 | tf_op jit(solution)/shard_map/odd_kernel/pallas_call | solution.py:473
  69.2 3.1 %collective-permute-done.20.recv_ref = bf16[128,512]{1,0:T(8,128)(2,1)S(1)} collective-permute-done((bf16[128,512]{1,0:T(8,128)(2,1)S(1)}, bf16[128,512]{1,0:T(8,128)(2,1)S(1)}, u32[]{:S(2)}, u32[]{:S(2)}) %collective-permute-start.20) | collective-permute-done | bytes 131104 | tf_op jit(solution)/shard_map/ppermute | solution.py:388
  75.4 1.8 %even_kernel.7 = (bf16[512,512]{1,0:T(8,128)(2,1)S(1)}, bf16[512,512]{1,0:T(8,128)(2,1)S(1)}) custom-call(bf16[512,512]{1,0:T(8,128)(2,1)S(1)} %get-tuple-element.117.x_ref, bf16[512,512]{1,0:T(8,128)(2,1)S(1)} %get-tuple-element.118.h_ref.refs_2_.refs_0_, bf16[512,512]{1,0:T(8,128)(2,1)S(1)} %get-tuple-element.74.adj_ref, ...), custom_call_target="tpu_custom_call" | custom-call | flops 134217728 | tf_op jit(solution)/shard_map/even_kernel/pallas_call | solution.py:463
  77.9 1.4 %collective-permute-done.23.dep.first_ref = bf16[528,512]{1,0:T(8,128)(2,1)S(1)} collective-permute-done((bf16[528,512]{1,0:T(8,128)(2,1)S(1)}, bf16[528,512]{1,0:T(8,128)(2,1)S(1)}, u32[]{:S(2)}, u32[]{:S(2)}) %collective-permute-start.23) | collective-permute-done | bytes 540704 | tf_op jit(solution)/shard_map/ppermute | solution.py:372
  79.4 1.4 %odd_kernel.7 = (f32[512,512]{1,0:T(8,128)S(1)}, bf16[512,512]{1,0:T(8,128)(2,1)S(1)}, bf16[128,512]{1,0:T(8,128)(2,1)S(1)}) custom-call(bf16[528,512]{1,0:T(8,128)(2,1)S(1)} %collective-permute-done.23.dep.first_ref, bf16[512,512]{1,0:T(8,128)(2,1)S(1)} %get-tuple-element.125.x_ref.refs_1_, bf16[512,512]{1,0:T(8,128)(2,1)S(1)} %get-tuple-element.74.adj_ref, ...), custom_call_target="tpu_custom_call" | custom-call | flops 5368709120 | tf_op jit(solution)/shard_map/odd_kernel/pallas_call | solution.py:473
  80.7 3.9 %collective-permute-done.22.recv_ref = bf16[128,512]{1,0:T(8,128)(2,1)S(1)} collective-permute-done((bf16[128,512]{1,0:T(8,128)(2,1)S(1)}, bf16[128,512]{1,0:T(8,128)(2,1)S(1)}, u32[]{:S(2)}, u32[]{:S(2)}) %collective-permute-start.22) | collective-permute-done | bytes 131104 | tf_op jit(solution)/shard_map/ppermute | solution.py:388
  86.8 2.6 %collective-permute-start.25 = (bf16[544,512]{1,0:T(8,128)(2,1)S(1)}, bf16[544,512]{1,0:T(8,128)(2,1)S(1)}, u32[]{:S(2)}, u32[]{:S(2)}) collective-permute-start(bf16[544,512]{1,0:T(8,128)(2,1)S(1)} %get-tuple-element.131), channel_id=1, source_target_pairs={{0,16},{1,17},{2,18},{3,19},{4,20},{5,21},{6,22},{7,23},{8,24},{9,... | collective-permute-start | bytes 1671176 | tf_op jit(solution)/shard_map/ppermute | solution.py:372
  90.1 1.3 %collective-permute-start.28 = (bf16[512,512]{1,0:T(8,128)(2,1)S(1)}, bf16[512,512]{1,0:T(8,128)(2,1)S(1)}, u32[]{:S(2)}, u32[]{:S(2)}) collective-permute-start(bf16[512,512]{1,0:T(8,128)(2,1)S(1)} %tie.11), channel_id=1, source_target_pairs={{8,24},{17,25},{10,26},{19,27},{12,28},{21,29},{14,30},{23,31}} | collective-permute-start | bytes 1572872 | tf_op jit(solution)/shard_map/ppermute | solution.py:510
  92.3 8.2 %collective-permute-done.24.one_ref = bf16[544,512]{1,0:T(8,128)(2,1)S(1)} collective-permute-done((bf16[544,512]{1,0:T(8,128)(2,1)S(1)}, bf16[544,512]{1,0:T(8,128)(2,1)S(1)}, u32[]{:S(2)}, u32[]{:S(2)}) %collective-permute-start.24) | collective-permute-done | bytes 557088 | tf_op jit(solution)/shard_map/ppermute | solution.py:372
  100.5 1.2 %collective-permute-done.25.two_ref = bf16[544,512]{1,0:T(8,128)(2,1)S(1)} collective-permute-done((bf16[544,512]{1,0:T(8,128)(2,1)S(1)}, bf16[544,512]{1,0:T(8,128)(2,1)S(1)}, u32[]{:S(2)}, u32[]{:S(2)}) %collective-permute-start.25) | collective-permute-done | bytes 557088 | tf_op jit(solution)/shard_map/ppermute | solution.py:372
  101.7 8.4 %collective-permute-done.28.three_ref = bf16[512,512]{1,0:T(8,128)(2,1)S(1)} collective-permute-done((bf16[512,512]{1,0:T(8,128)(2,1)S(1)}, bf16[512,512]{1,0:T(8,128)(2,1)S(1)}, u32[]{:S(2)}, u32[]{:S(2)}) %collective-permute-start.28) | collective-permute-done | bytes 524320 | tf_op jit(solution)/shard_map/ppermute | solution.py:510
  110.0 1.2 %collect_last_kernel.1 = bf16[1,4,512,512]{3,2,1,0:T(8,128)(2,1)} custom-call(bf16[544,512]{1,0:T(8,128)(2,1)S(1)} %collective-permute-done.24.one_ref, bf16[544,512]{1,0:T(8,128)(2,1)S(1)} %collective-permute-done.25.two_ref, bf16[512,512]{1,0:T(8,128)(2,1)S(1)} %collective-permute-done.28.three_ref, ...), custom_call_target="tpu_custom_call", output_to_operand_aliasing={{}: (6, {})} | custom-call | tf_op jit(solution)/shard_map/collect_last_kernel/pallas_call | solution.py:519
  (90 shorter events, 23.2 us)
Async XLA Ops:
  1.4 11.6 %copy-start.8 = (s32[2,128]{1,0:T(2,128)S(1)}, s32[2,128]{1,0:T(2,128)}, u32[]{:S(2)}) copy-start(s32[2,128]{1,0:T(2,128)} %param.17) | copy-start | bytes 3076
  1.4 11.5 %copy-start.6 = (f32[2,512]{1,0:T(2,128)S(1)}, f32[2,512]{1,0:T(2,128)}, u32[]{:S(2)}) copy-start(f32[2,512]{1,0:T(2,128)} %param.12) | copy-start | bytes 12292
  1.6 10.7 %collective-permute-start.1 = (bf16[640,512]{1,0:T(8,128)(2,1)S(1)}, bf16[640,512]{1,0:T(8,128)(2,1)S(1)}, u32[]{:S(2)}, u32[]{:S(2)}) collective-permute-start(bf16[640,512]{1,0:T(8,128)(2,1)S(1)} %get-tuple-element.70.refs_1_.refs_0_), channel_id=1, source_target_pairs={{0,8},{1,17},{2,10},{3,19},{4,12},{5,21},{6,14},{7,23},{8,0},{9,25... | collective-permute-start | bytes 1966088 | tf_op jit(solution)/shard_map/ppermute | solution.py:372
  2.2 23.3 %collective-permute-start = (bf16[640,512]{1,0:T(8,128)(2,1)S(1)}, bf16[640,512]{1,0:T(8,128)(2,1)S(1)}, u32[]{:S(2)}, u32[]{:S(2)}) collective-permute-start(bf16[640,512]{1,0:T(8,128)(2,1)S(1)} %get-tuple-element.69.refs_1_.refs_0_), channel_id=1, source_target_pairs={{0,8},{1,17},{2,10},{3,19},{4,12},{5,21},{6,14},{7,23},{8,0},{9,25... | collective-permute-start | bytes 1966088 | tf_op jit(solution)/shard_map/ppermute | solution.py:372
  12.3 14.7 %collective-permute-start.6 = (bf16[640,512]{1,0:T(8,128)(2,1)S(1)}, bf16[640,512]{1,0:T(8,128)(2,1)S(1)}, u32[]{:S(2)}, u32[]{:S(2)}) collective-permute-start(bf16[640,512]{1,0:T(8,128)(2,1)S(1)} %select_kernel.6.refs_2_), channel_id=1, source_target_pairs={{0,16},{1,9},{2,18},{3,11},{4,20},{5,13},{6,22},{7,15},{8,24},{9,1... | collective-permute-start | bytes 1966088 | tf_op jit(solution)/shard_map/ppermute | solution.py:372
  12.9 11.8 %collective-permute-start.4 = (f32[2,1152]{1,0:T(2,128)S(1)}, f32[2,1152]{1,0:T(2,128)S(1)}, u32[]{:S(2)}, u32[]{:S(2)}) collective-permute-start(f32[2,1152]{1,0:T(2,128)S(1)} %tie.6.s0), channel_id=1, source_target_pairs={{0,24},{1,25},{2,26},{3,27},{4,28},{5,29},{6,30},{7,31},{8,16},{9,... | collective-permute-start | bytes 27656 | tf_op jit(solution)/shard_map/ppermute | solution.py:372
  14.5 11.0 %collective-permute-start.3 = (f32[2,1152]{1,0:T(2,128)S(1)}, f32[2,1152]{1,0:T(2,128)S(1)}, u32[]{:S(2)}, u32[]{:S(2)}) collective-permute-start(f32[2,1152]{1,0:T(2,128)S(1)} %tie.6.s0), channel_id=1, source_target_pairs={{0,16},{1,17},{2,18},{3,19},{4,20},{5,21},{6,22},{7,23},{8,24},{9,... | collective-permute-start | bytes 27656 | tf_op jit(solution)/shard_map/ppermute | solution.py:372
  14.6 10.9 %collective-permute-start.2 = (f32[2,1152]{1,0:T(2,128)S(1)}, f32[2,1152]{1,0:T(2,128)S(1)}, u32[]{:S(2)}, u32[]{:S(2)}) collective-permute-start(f32[2,1152]{1,0:T(2,128)S(1)} %tie.6.s0), channel_id=1, source_target_pairs={{0,8},{1,9},{2,10},{3,11},{4,12},{5,13},{6,14},{7,15},{8,0},{9,1},... | collective-permute-start | bytes 27656 | tf_op jit(solution)/shard_map/ppermute | solution.py:372
  25.6 10.7 %collective-permute-start.11 = (bf16[640,512]{1,0:T(8,128)(2,1)S(1)}, bf16[640,512]{1,0:T(8,128)(2,1)S(1)}, u32[]{:S(2)}, u32[]{:S(2)}) collective-permute-start(bf16[640,512]{1,0:T(8,128)(2,1)S(1)} %select_kernel.7.dep.refs_2_), channel_id=1, source_target_pairs={{0,16},{1,9},{2,18},{3,11},{4,20},{5,13},{6,22},{7,15},{8,24},{9,1... | collective-permute-start | bytes 1966088 | tf_op jit(solution)/shard_map/ppermute | solution.py:372
  26.5 5.2 %collective-permute-start.7 = (bf16[512,512]{1,0:T(8,128)(2,1)S(1)}, bf16[512,512]{1,0:T(8,128)(2,1)S(1)}, u32[]{:S(2)}, u32[]{:S(2)}) collective-permute-start(bf16[512,512]{1,0:T(8,128)(2,1)S(1)} %top_kernel.3), channel_id=1, source_target_pairs={{0,1},{1,0},{2,3},{3,2},{4,5},{5,4},{6,7},{7,6},{8,9},{9,8},{10,11... | collective-permute-start | bytes 1572872 | tf_op jit(solution)/shard_map/ppermute | solution.py:372
  27.1 4.6 %collective-permute-start.8 = (bf16[512,512]{1,0:T(8,128)(2,1)S(1)}, bf16[512,512]{1,0:T(8,128)(2,1)S(1)}, u32[]{:S(2)}, u32[]{:S(2)}) collective-permute-start(bf16[512,512]{1,0:T(8,128)(2,1)S(1)} %top_kernel.4), channel_id=1, source_target_pairs={{0,1},{1,0},{2,3},{3,2},{4,5},{5,4},{6,7},{7,6},{8,9},{9,8},{10,11... | collective-permute-start | bytes 1572872 | tf_op jit(solution)/shard_map/ppermute | solution.py:372
  29.0 3.7 %collective-permute-start.5 = (bf16[128,512]{1,0:T(8,128)(2,1)S(1)}, bf16[128,512]{1,0:T(8,128)(2,1)S(1)}, u32[]{:S(2)}, u32[]{:S(2)}) collective-permute-start(bf16[128,512]{1,0:T(8,128)(2,1)S(1)} %get-tuple-element.71), channel_id=1, source_target_pairs={{0,1},{1,0},{2,3},{3,2},{4,5},{5,4},{6,7},{7,6},{8,9},{9,8},{10,11... | collective-permute-start | bytes 393224 | tf_op jit(solution)/shard_map/ppermute | solution.py:388
  30.2 13.1 %collective-permute-start.10 = (bf16[640,512]{1,0:T(8,128)(2,1)S(1)}, bf16[640,512]{1,0:T(8,128)(2,1)S(1)}, u32[]{:S(2)}, u32[]{:S(2)}) collective-permute-start(bf16[640,512]{1,0:T(8,128)(2,1)S(1)} %select_kernel.8.refs_2_), channel_id=1, source_target_pairs={{0,16},{1,9},{2,18},{3,11},{4,20},{5,13},{6,22},{7,15},{8,24},{9,1... | collective-permute-start | bytes 1966088 | tf_op jit(solution)/shard_map/ppermute | solution.py:372
  33.3 10.0 %collective-permute-start.12 = (bf16[640,512]{1,0:T(8,128)(2,1)S(1)}, bf16[640,512]{1,0:T(8,128)(2,1)S(1)}, u32[]{:S(2)}, u32[]{:S(2)}) collective-permute-start(bf16[640,512]{1,0:T(8,128)(2,1)S(1)} %tie.7.refs_2_), channel_id=1, source_target_pairs={{0,1},{1,0},{2,3},{3,2},{4,5},{5,4},{6,7},{7,6},{8,9},{9,8},{10,11... | collective-permute-start | bytes 1966088 | tf_op jit(solution)/shard_map/ppermute | solution.py:372
  36.2 7.0 %collective-permute-start.13 = (bf16[640,512]{1,0:T(8,128)(2,1)S(1)}, bf16[640,512]{1,0:T(8,128)(2,1)S(1)}, u32[]{:S(2)}, u32[]{:S(2)}) collective-permute-start(bf16[640,512]{1,0:T(8,128)(2,1)S(1)} %tie.8.refs_3_), channel_id=1, source_target_pairs={{0,1},{1,0},{2,3},{3,2},{4,5},{5,4},{6,7},{7,6},{8,9},{9,8},{10,11... | collective-permute-start | bytes 1966088 | tf_op jit(solution)/shard_map/ppermute | solution.py:372
  36.4 9.4 %collective-permute-start.9 = (bf16[128,512]{1,0:T(8,128)(2,1)S(1)}, bf16[128,512]{1,0:T(8,128)(2,1)S(1)}, u32[]{:S(2)}, u32[]{:S(2)}) collective-permute-start(bf16[128,512]{1,0:T(8,128)(2,1)S(1)} %send_kernel.4.dep.refs_1_), channel_id=1, source_target_pairs={{0,4},{1,5},{2,6},{3,7},{4,0},{5,1},{6,2},{7,3},{8,12},{9,13},{10,... | collective-permute-start | bytes 393224 | tf_op jit(solution)/shard_map/ppermute | solution.py:388
  39.0 11.3 %collective-permute-start.17 = (bf16[640,512]{1,0:T(8,128)(2,1)S(1)}, bf16[640,512]{1,0:T(8,128)(2,1)S(1)}, u32[]{:S(2)}, u32[]{:S(2)}) collective-permute-start(bf16[640,512]{1,0:T(8,128)(2,1)S(1)} %select_kernel.9.dep), channel_id=1, source_target_pairs={{0,16},{1,9},{2,18},{3,11},{4,20},{5,13},{6,22},{7,15},{8,24},{9,1... | collective-permute-start | bytes 1966088 | tf_op jit(solution)/shard_map/ppermute | solution.py:372
  45.9 2.0 %collective-permute-start.15 = (bf16[512,512]{1,0:T(8,128)(2,1)S(1)}, bf16[512,512]{1,0:T(8,128)(2,1)S(1)}, u32[]{:S(2)}, u32[]{:S(2)}) collective-permute-start(bf16[512,512]{1,0:T(8,128)(2,1)S(1)} %top_kernel.5), channel_id=1, source_target_pairs={{0,1},{1,0},{2,3},{3,2},{4,5},{5,4},{6,7},{7,6},{8,9},{9,8},{10,11... | collective-permute-start | bytes 1572872 | tf_op jit(solution)/shard_map/ppermute | solution.py:372
  47.1 1.8 %collective-permute-start.14 = (bf16[128,512]{1,0:T(8,128)(2,1)S(1)}, bf16[128,512]{1,0:T(8,128)(2,1)S(1)}, u32[]{:S(2)}, u32[]{:S(2)}) collective-permute-start(bf16[128,512]{1,0:T(8,128)(2,1)S(1)} %get-tuple-element.88), channel_id=1, source_target_pairs={{0,1},{1,0},{2,3},{3,2},{4,5},{5,4},{6,7},{7,6},{8,9},{9,8},{10,11... | collective-permute-start | bytes 393224 | tf_op jit(solution)/shard_map/ppermute | solution.py:388
  50.3 4.5 %collective-permute-start.18 = (bf16[640,512]{1,0:T(8,128)(2,1)S(1)}, bf16[640,512]{1,0:T(8,128)(2,1)S(1)}, u32[]{:S(2)}, u32[]{:S(2)}) collective-permute-start(bf16[640,512]{1,0:T(8,128)(2,1)S(1)} %tie.10.refs_4_), channel_id=1, source_target_pairs={{0,1},{1,0},{2,3},{3,2},{4,5},{5,4},{6,7},{7,6},{8,9},{9,8},{10,11... | collective-permute-start | bytes 1966088 | tf_op jit(solution)/shard_map/ppermute | solution.py:372
  50.4 9.5 %collective-permute-start.16 = (bf16[128,512]{1,0:T(8,128)(2,1)S(1)}, bf16[128,512]{1,0:T(8,128)(2,1)S(1)}, u32[]{:S(2)}, u32[]{:S(2)}) collective-permute-start(bf16[128,512]{1,0:T(8,128)(2,1)S(1)} %send_kernel.5.dep.refs_1_), channel_id=1, source_target_pairs={{0,4},{1,5},{2,6},{3,7},{4,0},{5,1},{6,2},{7,3},{8,12},{9,13},{10,... | collective-permute-start | bytes 393224 | tf_op jit(solution)/shard_map/ppermute | solution.py:388
  61.0 1.4 %collective-permute-start.19 = (bf16[128,512]{1,0:T(8,128)(2,1)S(1)}, bf16[128,512]{1,0:T(8,128)(2,1)S(1)}, u32[]{:S(2)}, u32[]{:S(2)}) collective-permute-start(bf16[128,512]{1,0:T(8,128)(2,1)S(1)} %get-tuple-element.102), channel_id=1, source_target_pairs={{0,1},{1,0},{2,3},{3,2},{4,5},{5,4},{6,7},{7,6},{8,9},{9,8},{10,11... | collective-permute-start | bytes 393224 | tf_op jit(solution)/shard_map/ppermute | solution.py:388
  63.0 9.3 %collective-permute-start.20 = (bf16[128,512]{1,0:T(8,128)(2,1)S(1)}, bf16[128,512]{1,0:T(8,128)(2,1)S(1)}, u32[]{:S(2)}, u32[]{:S(2)}) collective-permute-start(bf16[128,512]{1,0:T(8,128)(2,1)S(1)} %send_kernel.6.dep), channel_id=1, source_target_pairs={{0,4},{1,5},{2,6},{3,7},{4,0},{5,1},{6,2},{7,3},{8,12},{9,13},{10,... | collective-permute-start | bytes 393224 | tf_op jit(solution)/shard_map/ppermute | solution.py:388
  64.9 14.5 %collective-permute-start.23 = (bf16[528,512]{1,0:T(8,128)(2,1)S(1)}, bf16[528,512]{1,0:T(8,128)(2,1)S(1)}, u32[]{:S(2)}, u32[]{:S(2)}) collective-permute-start(bf16[528,512]{1,0:T(8,128)(2,1)S(1)} %select_kernel.10), channel_id=1, source_target_pairs={{24,0},{25,1},{26,2},{27,3},{28,4},{29,5},{30,6},{31,7},{16,8},{17... | collective-permute-start | bytes 1622024 | tf_op jit(solution)/shard_map/ppermute | solution.py:372
  73.4 1.4 %collective-permute-start.21 = (bf16[128,512]{1,0:T(8,128)(2,1)S(1)}, bf16[128,512]{1,0:T(8,128)(2,1)S(1)}, u32[]{:S(2)}, u32[]{:S(2)}) collective-permute-start(bf16[128,512]{1,0:T(8,128)(2,1)S(1)} %get-tuple-element.116), channel_id=1, source_target_pairs={{0,1},{1,0},{2,3},{3,2},{4,5},{5,4},{6,7},{7,6},{8,9},{9,8},{10,11... | collective-permute-start | bytes 393224 | tf_op jit(solution)/shard_map/ppermute | solution.py:388
  75.3 9.3 %collective-permute-start.22 = (bf16[128,512]{1,0:T(8,128)(2,1)S(1)}, bf16[128,512]{1,0:T(8,128)(2,1)S(1)}, u32[]{:S(2)}, u32[]{:S(2)}) collective-permute-start(bf16[128,512]{1,0:T(8,128)(2,1)S(1)} %send_kernel.7.dep), channel_id=1, source_target_pairs={{0,4},{1,5},{2,6},{3,7},{4,0},{5,1},{6,2},{7,3},{8,12},{9,13},{10,... | collective-permute-start | bytes 393224 | tf_op jit(solution)/shard_map/ppermute | solution.py:388
  77.2 12.2 %collective-permute-start.27 = (bf16[528,512]{1,0:T(8,128)(2,1)S(1)}, bf16[528,512]{1,0:T(8,128)(2,1)S(1)}, u32[]{:S(2)}, u32[]{:S(2)}) collective-permute-start(bf16[528,512]{1,0:T(8,128)(2,1)S(1)} %select_kernel.11), channel_id=1, source_target_pairs={{8,16},{9,25},{10,18},{11,27},{12,20},{13,29},{14,22},{15,31}} | collective-permute-start | bytes 1622024 | tf_op jit(solution)/shard_map/ppermute | solution.py:372
  85.6 4.6 %collective-permute-start.26 = (bf16[512,512]{1,0:T(8,128)(2,1)S(1)}, bf16[512,512]{1,0:T(8,128)(2,1)S(1)}, u32[]{:S(2)}, u32[]{:S(2)}) collective-permute-start(bf16[512,512]{1,0:T(8,128)(2,1)S(1)} %get-tuple-element.132.refs_3_), channel_id=1, source_target_pairs={{0,8},{1,17},{2,10},{3,19},{4,12},{5,21},{6,14},{7,23}} | collective-permute-start | bytes 1572872 | tf_op jit(solution)/shard_map/ppermute | solution.py:372
  86.3 14.2 %collective-permute-start.24 = (bf16[544,512]{1,0:T(8,128)(2,1)S(1)}, bf16[544,512]{1,0:T(8,128)(2,1)S(1)}, u32[]{:S(2)}, u32[]{:S(2)}) collective-permute-start(bf16[544,512]{1,0:T(8,128)(2,1)S(1)} %get-tuple-element.130), channel_id=1, source_target_pairs={{0,8},{1,9},{2,10},{3,11},{4,12},{5,13},{6,14},{7,15},{8,0},{9,1},... | collective-permute-start | bytes 1671176 | tf_op jit(solution)/shard_map/ppermute | solution.py:372
  86.8 14.8 %collective-permute-start.25 = (bf16[544,512]{1,0:T(8,128)(2,1)S(1)}, bf16[544,512]{1,0:T(8,128)(2,1)S(1)}, u32[]{:S(2)}, u32[]{:S(2)}) collective-permute-start(bf16[544,512]{1,0:T(8,128)(2,1)S(1)} %get-tuple-element.131), channel_id=1, source_target_pairs={{0,16},{1,17},{2,18},{3,19},{4,20},{5,21},{6,22},{7,23},{8,24},{9,... | collective-permute-start | bytes 1671176 | tf_op jit(solution)/shard_map/ppermute | solution.py:372
  89.4 12.2 %collective-permute-start.29 = (bf16[528,512]{1,0:T(8,128)(2,1)S(1)}, bf16[528,512]{1,0:T(8,128)(2,1)S(1)}, u32[]{:S(2)}, u32[]{:S(2)}) collective-permute-start(bf16[528,512]{1,0:T(8,128)(2,1)S(1)} %collective-permute-done.27.refs_1_.early_ref), channel_id=1, source_target_pairs={{25,17},{27,19},{29,21},{31,23}} | collective-permute-start | bytes 1622024 | tf_op jit(solution)/shard_map/ppermute | solution.py:510
  90.1 19.9 %collective-permute-start.28 = (bf16[512,512]{1,0:T(8,128)(2,1)S(1)}, bf16[512,512]{1,0:T(8,128)(2,1)S(1)}, u32[]{:S(2)}, u32[]{:S(2)}) collective-permute-start(bf16[512,512]{1,0:T(8,128)(2,1)S(1)} %tie.11), channel_id=1, source_target_pairs={{8,24},{17,25},{10,26},{19,27},{12,28},{21,29},{14,30},{23,31}} | collective-permute-start | bytes 1572872 | tf_op jit(solution)/shard_map/ppermute | solution.py:510
  (7 other events, 22.2 us)
